TPU v7x, 32 devices: a whole 2x2x4 slice. The times are simulated.
32 devices in a mesh: group: 1, wide: 32 (over z, y, x, core).
Axes of the slice: x: 2, y: 2, z: 4, core: 2. Of those that a mesh axis runs over, the one named last changes fastest.
Arguments:
- ssd_x: bfloat16 [2048, 4096], P(('group', 'wide')), may hold values from -6 to 6
- ssd_z: bfloat16 [2048, 4096], P(('group', 'wide')), may hold values from -6 to 6
- ssd_b: bfloat16 [2048, 128], P(('group', 'wide')), may hold values from -2 to 2
- ssd_c: bfloat16 [2048, 128], P(('group', 'wide')), may hold values from -2 to 2
- dt_raw: bfloat16 [2048, 64], P(('group', 'wide')), may hold values from -4 to 4
- dt_bias: float32 [64], replicated, may hold values from -4 to -1
- a_log: float32 [64], replicated, may hold values from -1.5 to 1.5
- d_skip: float32 [64], replicated, may hold values from 0.5 to 1.5
- norm_gain: float32 [4096], replicated, may hold values from 0.1 to 1.9
- cache_state: bfloat16 [64, 64, 64, 128], P(('group', 'wide')), may hold values from -2 to 2
- cache_owner: int32 [64], P('group'), may hold values from 0 to 63
- resid: bfloat16 [2048, 2048], P(('group', 'wide')), may hold values from -3 to 3
- w_out: bfloat16 [4096, 2048], P('wide'), may hold values from -0.09375 to 0.09375
- moe_gain: float32 [2048], replicated, may hold values from 0.1 to 1.9
- expert_ids: int32 [2048, 10], P(('group', 'wide')), may hold values from 0 to 31, all different within a row; in each aligned block of 64 rows (0 to 63, 64 to 127, ...) at most 32 rows name the same one
- route_weight: int32 [2048, 10], P(('group', 'wide')), may hold values from 1 to 1023
- expert_home: int32 [32], replicated, may hold values from 0 to 31, each once
- w_gate: bfloat16 [32, 2048, 384], P('wide'), may hold values from -0.125 to 0.125
- w_up: bfloat16 [32, 2048, 384], P('wide'), may hold values from -0.125 to 0.125
- w_down: bfloat16 [32, 384, 2048], P('wide'), may hold values from -0.3125 to 0.3125
Outputs:
- ssd_out: bfloat16 [2048, 4096], P(('group', 'wide'))
- moe_out: bfloat16 [2048, 2048], P(('group', 'wide'))
Inputs may be any that keep to these rules, and one draw needn't show every extreme that they name: `cache_owner`: slot s of cache_state holds a cached prefix state; several requests may continue from the same slot. `expert_ids`: each token names 10 different experts. In each aligned block of 64 tokens (the tokens of one device) no expert is named by more than 32 tokens, and in every draw some expert is named by exactly 32 tokens of some block. `expert_home`: A permutation of the experts.
All inputs are finite; a program needn't handle non-finite values.
Results may differ from a plain program's by a relative error of at most 0.02.
Values may be sent and summed in bfloat16 or wider, within the bound.
A program may use at most 128 MiB of HBM per device.

v0:
```python
import jax
import jax.numpy as jnp
from jax import lax
from jax.sharding import PartitionSpec as P

SEQ = 32


def intra_terms(inputs, step_size, cumulative, b_proj, c_proj, skip_gain):
    scores = jnp.einsum("rtn,rsn->rts", c_proj, b_proj, preferred_element_type=jnp.float32)
    length = inputs.shape[1]
    causal = jnp.arange(length)[:, None] >= jnp.arange(length)[None, :]
    cum_heads = jnp.swapaxes(cumulative, 1, 2)
    log_gap = cum_heads[..., :, None] - cum_heads[..., None, :]
    decays = jnp.where(causal, jnp.exp(jnp.where(causal, log_gap, 0.0)), 0.0)
    mixing = (scores[:, None] * decays * jnp.swapaxes(step_size, 1, 2)[:, :, None, :]).astype(
        jnp.bfloat16
    )
    result = jnp.einsum("rhts,rshp->rthp", mixing, inputs, preferred_element_type=jnp.float32)
    result = result + skip_gain[None, None, :, None] * inputs.astype(jnp.float32)
    return result.astype(jnp.bfloat16)


def state_terms(c_proj, cumulative, start_state):
    product = jnp.einsum("rtn,rhpn->rthp", c_proj, start_state, preferred_element_type=jnp.float32)
    return (product * jnp.exp(cumulative)[..., None]).astype(jnp.bfloat16)


def expert_mlp(row_set, gate_weight, up_weight, down_weight):
    gate_out = jnp.dot(row_set, gate_weight, preferred_element_type=jnp.float32)
    up_out = jnp.dot(row_set, up_weight, preferred_element_type=jnp.float32)
    hidden = (jax.nn.silu(gate_out) * up_out).astype(jnp.bfloat16)
    return jnp.dot(hidden, down_weight, preferred_element_type=jnp.float32).astype(jnp.bfloat16)


def head_steps(raw_steps, bias_part, rate_part, requests):
    step_size = jax.nn.softplus(raw_steps.astype(jnp.float32) + bias_part)
    step_size = step_size.reshape(requests, SEQ, step_size.shape[-1])
    return (step_size, jnp.cumsum(step_size * rate_part, axis=1))


def local(
    ssd_x,
    ssd_z,
    ssd_b,
    ssd_c,
    dt_raw,
    dt_bias,
    a_log,
    d_skip,
    norm_gain,
    cache_state,
    cache_owner,
    resid,
    w_out,
    moe_gain,
    expert_ids,
    route_weight,
    expert_home,
    w_gate,
    w_up,
    w_down,
):
    devices = lax.axis_size("wide")
    my_index = lax.axis_index("wide")
    tok_dev = ssd_x.shape[0]
    heads_all = dt_raw.shape[1]
    per_dev = heads_all // devices
    head_dim = ssd_x.shape[1] // heads_all
    state_size = ssd_b.shape[1]
    req_local = tok_dev // SEQ
    rates = -jnp.exp(a_log)
    bias_part = lax.dynamic_slice_in_dim(dt_bias, my_index * per_dev, per_dev)
    rate_part = lax.dynamic_slice_in_dim(rates, my_index * per_dev, per_dev)
    by_heads = lax.all_to_all(cache_state, "wide", split_axis=1, concat_axis=0, tiled=True)
    start_state = jnp.take(by_heads, cache_owner, axis=0)
    requests = cache_owner.shape[0]
    tokens_all = requests * SEQ
    local_step, local_cum = head_steps(dt_raw, dt_bias, rates, req_local)
    intra = intra_terms(
        ssd_x.reshape(req_local, SEQ, heads_all, head_dim),
        local_step,
        local_cum,
        ssd_b.reshape(req_local, SEQ, state_size),
        ssd_c.reshape(req_local, SEQ, state_size),
        d_skip,
    )
    intra = intra.reshape(tok_dev, heads_all * head_dim)
    c_all = lax.all_gather(ssd_c, "wide", axis=0, tiled=True)
    head_raw = lax.all_to_all(dt_raw, "wide", split_axis=1, concat_axis=0, tiled=True)
    step_size, cumulative = head_steps(head_raw, bias_part, rate_part, requests)
    carried_head = state_terms(c_all.reshape(requests, SEQ, state_size), cumulative, start_state)
    carried = lax.all_to_all(
        carried_head.reshape(tokens_all, per_dev * head_dim),
        "wide",
        split_axis=0,
        concat_axis=1,
        tiled=True,
    )
    mixed = intra.astype(jnp.float32) + carried.astype(jnp.float32)
    gated = mixed * jax.nn.silu(ssd_z.astype(jnp.float32))
    ssd_out = (
        gated * lax.rsqrt(jnp.mean(gated * gated, axis=-1, keepdims=True) + 1e-05) * norm_gain
    ).astype(jnp.bfloat16)
    width = resid.shape[1]
    projected = jnp.dot(
        ssd_out,
        lax.all_gather(w_out, "wide", axis=0, tiled=True),
        preferred_element_type=jnp.float32,
    )
    topk = expert_ids.shape[1]
    expert_count = expert_home.shape[0]
    wide_moe = resid.astype(jnp.float32) + projected
    normed = (
        wide_moe
        * lax.rsqrt(jnp.mean(wide_moe * wide_moe, axis=-1, keepdims=True) + 1e-05)
        * moe_gain
    ).astype(jnp.bfloat16)
    weight_f = route_weight.astype(jnp.float32)
    share = weight_f / jnp.sum(weight_f, axis=-1, keepdims=True)
    lookup = expert_ids[..., None] == jnp.arange(expert_count, dtype=jnp.int32)
    target = jnp.sum(jnp.where(lookup, expert_home, 0), axis=-1)
    pair_count = tok_dev * topk
    flat_target = target.reshape(pair_count)
    one_hot = (flat_target[:, None] == jnp.arange(devices, dtype=jnp.int32)).astype(jnp.int32)
    before = jnp.cumsum(one_hot, axis=0) - one_hot
    slot_of = jnp.sum(before * one_hot, axis=-1)
    capacity = tok_dev * topk // expert_count * 8 // 5
    position = flat_target * capacity + slot_of
    source_row = (
        jnp.zeros((devices * capacity,), jnp.int32)
        .at[position]
        .set(jnp.arange(pair_count, dtype=jnp.int32) // topk + 1)
    )
    filled = source_row > 0
    fetched = jnp.take(normed, jnp.maximum(source_row - 1, 0), axis=0)
    send_rows = jnp.where(filled[:, None], fetched, jnp.zeros((), jnp.bfloat16)).reshape(
        devices, capacity, width
    )
    received = lax.all_to_all(send_rows, "wide", split_axis=0, concat_axis=0, tiled=True)
    flat_rows = received.reshape(-1, received.shape[-1])
    outputs = expert_mlp(flat_rows, w_gate[0], w_up[0], w_down[0]).reshape(received.shape)
    returned = lax.all_to_all(outputs, "wide", split_axis=0, concat_axis=0, tiled=True)
    gathered = jnp.take(returned.reshape(devices * capacity, width), position, axis=0).reshape(
        tok_dev, topk, width
    )
    moe_out = jnp.sum(gathered.astype(jnp.float32) * share[..., None], axis=1).astype(jnp.bfloat16)
    return (ssd_out, moe_out)


def solution(mesh):
    in_specs = (
        P(("group", "wide"), None),
        P(("group", "wide"), None),
        P(("group", "wide"), None),
        P(("group", "wide"), None),
        P(("group", "wide"), None),
        P(),
        P(),
        P(),
        P(),
        P(("group", "wide"), None, None, None),
        P("group"),
        P(("group", "wide"), None),
        P("wide", None),
        P(),
        P(("group", "wide"), None),
        P(("group", "wide"), None),
        P(),
        P("wide", None, None),
        P("wide", None, None),
        P("wide", None, None),
    )
    out_specs = (P(("group", "wide"), None), P(("group", "wide"), None))
    return jax.shard_map(local, mesh=mesh, in_specs=in_specs, out_specs=out_specs, check_vma=False)
```

profile of v0, /device:TPU:0, one launch (start us, length us, event | category | flops | bytes accessed | tf_op | source)
XLA Modules:
  0.0 430.1 jit_solution(291242435058443857)
XLA Ops:
  7.2 0.0 copy-start
  7.2 0.0 all-gather.2.cloned.1.call-start
  7.2 0.7 all-gather.2.cloned.1.call-update
  7.9 1.4 copy.108
  9.3 7.3 %all-to-all-start.1 = ((bf16[64,32,2]{0,2,1:T(2,128)(2,1)}), bf16[64,32,2]{0,2,1:T(2,128)(2,1)S(1)}, u32[]{:S(2)}, u32[]{:S(2)}) async-start(bf16[64,32,2]{0,2,1:T(2,128)(2,1)} %bitcast.14), calls=%async_computation.1 | async-start | bytes 32768 | tf_op jit(solution)/shard_map/all_to_all | solution.py:90
  16.6 3.1 copy.105
  19.8 3.9 all-to-all-done.1
  23.7 3.5 all-to-all-start
  27.2 0.1 select_reduce_fusion
  27.3 0.1 copy.115
  27.4 0.1 eq.42
  27.6 0.1 reshape.191
  27.7 0.1 dynamic_slice.7
  27.8 0.1 dynamic_slice.6
  27.9 0.1 reduce_window_sum.37
  28.0 0.1 copy.99
  28.1 0.1 copy.101
  28.2 1.1 reshape.189
  29.4 0.1 fusion.47
  29.5 1.9 fusion.12
  31.4 2.5 copy.104
  34.0 2.1 reshape.196
  36.1 1.5 reduce-window.6
  37.6 0.3 slice_reduce_fusion
  37.9 84.0 %all_gather.6 = bf16[2048,128]{1,0:T(8,128)(2,1)S(1)} all-gather(bf16[64,128]{1,0:T(8,128)(2,1)S(1)} %copy-done.6), channel_id=1, replica_groups=mesh['group'=1,'wide'=32] {'wide'}, dimensions={0}, use_global_device_ids=true | all-gather | bytes 540672 | tf_op jit(solution)/shard_map/all_gather | solution.py:89
  122.0 0.1 reshape.197
  122.1 0.1 copy.110
  122.1 0.1 fusion.33
  122.2 1.4 copy.111
  123.6 2.4 reduce-window_exponential_fusion
  126.0 1.9 copy.112
  127.9 3.2 copy.107
  131.1 3.8 gather_fusion
  134.8 3.7 fusion
  138.5 2.1 copy.113
  140.6 3.2 all_to_all.45
  143.8 15.1 %all-to-all-start.2 = ((bf16[32,64,128]{2,1,0:T(8,128)(2,1)}), bf16[32,64,128]{2,1,0:T(8,128)(2,1)S(1)}, u32[]{:S(2)}, u32[]{:S(2)}) async-start(bf16[32,64,128]{2,1,0:T(8,128)(2,1)} %all_to_all.45), calls=%async_computation.2 | async-start | bytes 1048576 | tf_op jit(solution)/shard_map/all_to_all | solution.py:93
  158.9 0.1 copy.120
  159.0 0.1 mul.161
  159.2 0.1 fusion.31
  159.3 4.1 scatter_custom_fusion
  163.4 0.1 broadcast_in_dim.101
  163.5 0.1 broadcast_in_dim.103
  163.6 10.9 %all-to-all-done.2 = bf16[32,64,128]{2,1,0:T(8,128)(2,1)S(1)} async-done(((bf16[32,64,128]{2,1,0:T(8,128)(2,1)}), bf16[32,64,128]{2,1,0:T(8,128)(2,1)S(1)}, u32[]{:S(2)}, u32[]{:S(2)}) %all-to-all-start.2) | async-done | bytes 524320 | tf_op jit(solution)/shard_map/all_to_all | solution.py:93
  174.4 1.5 multiply_reduce_fusion.1
  176.0 0.2 multiply_convert_fusion.3
  176.2 0.0 all-gather.2.cloned.1.call-done
  176.2 9.1 %multiply_reduce_fusion.2 = (f32[64]{0:T(128)S(1)}, f32[64,2048]{1,0:T(8,128)S(1)}) fusion(bf16[64,4096]{1,0:T(8,128)(2,1)S(1)} %multiply_convert_fusion.3, bf16[4096,2048]{1,0:T(8,128)(2,1)} %all-gather.2.cloned.1.call-done, bf16[64,2048]{1,0:T(8,128)(2,1)S(1)} %copy-done.4), kind=kOutput, calls=%fused_computation.42 | convolution fusion | flops 1074266112 | bytes 18088192 | tf_op jit(solution)/shard_map/dot_general | solution.py:106
  185.3 0.1 multiply_convert_fusion.4
  185.4 6.0 %gather_fusion.1 = bf16[1024,2048]{1,0:T(8,128)(2,1)} fusion(bf16[64,2048]{1,0:T(8,128)(2,1)S(1)} %multiply_convert_fusion.4, s32[1024]{0:T(1024)S(1)} %fusion.38), kind=kCustom, calls=%fused_computation.1 | custom fusion | bytes 8392704 | tf_op jit(solution)/shard_map/jit(_take)/gather | solution.py:136
  191.5 2.6 select_select_fusion
  194.1 96.5 %all_to_all.54 = bf16[32,32,2048]{2,1,0:T(8,128)(2,1)S(1)} all-to-all(bf16[32,32,2048]{2,1,0:T(8,128)(2,1)S(1)} %select_select_fusion), channel_id=1, replica_groups=mesh['group'=1,'wide'=32] {'wide'}, dimensions={0} | all-to-all | bytes 8388608 | tf_op jit(solution)/shard_map/all_to_all | solution.py:140
  290.6 2.0 copy-done.1
  292.6 3.6 fusion.8
  296.1 7.8 %convolution_convert_fusion = bf16[1024,2048]{1,0:T(8,128)(2,1)} fusion(bf16[1,384,2048]{2,1,0:T(8,128)(2,1)S(1)} %copy-done, f32[1024,384]{1,0:T(8,128)} %fusion.8, bf16[1024,2048]{1,0:T(8,128)(2,1)} %bitcast.90, bf16[1,2048,384]{2,1,0:T(8,128)(2,1)S(1)} %copy-done.15), kind=kOutput, calls=%fused_computation.6 | convolution fusion | flops 3225681920 | bytes 13107200 | tf_op jit(solution)/shard_map/dot_general | solution.py:33
  303.9 4.1 all-to-all-start.4
  308.0 0.1 reduce_sum.61
  308.1 0.1 copy.118
  308.2 0.1 copy.119
  308.4 0.1 copy.121
  308.5 93.3 %all-to-all-done.4 = bf16[32,32,2048]{2,1,0:T(8,128)(2,1)} async-done(((bf16[32,32,2048]{2,1,0:T(8,128)(2,1)}), bf16[32,32,2048]{2,1,0:T(8,128)(2,1)}, u32[]{:S(2)}, u32[]{:S(2)}) %all-to-all-start.4) | async-done | bytes 4194336 | tf_op jit(solution)/shard_map/all_to_all | solution.py:143
  401.8 9.7 %gather_fusion.2 = bf16[640,2048]{1,0:T(8,128)(2,1)} fusion(bf16[1024,2048]{1,0:T(8,128)(2,1)} %bitcast.24, s32[1024]{0:T(1024)S(1)} %pad_clamp_fusion), kind=kCustom, calls=%fused_computation.2 | custom fusion | bytes 5245440 | tf_op jit(solution)/shard_map/jit(_take)/gather | solution.py:144
  411.5 5.4 %gather.20 = bf16[64,10,2048]{2,1,0:T(8,128)(2,1)} reshape(bf16[640,2048]{1,0:T(8,128)(2,1)} %gather_fusion.2) | data formatting | bytes 5242880 | tf_op jit(solution)/shard_map/jit(_take)/gather | solution.py:144
  416.9 6.4 %multiply_reduce_fusion = bf16[64,2048]{1,0:T(8,128)(2,1)} fusion(f32[64,10]{1,0:T(8,128)S(1)} %copy.121, bf16[64,10,2048]{2,1,0:T(8,128)(2,1)} %gather.20, pred[64,10]{1,0:T(8,128)(4,1)S(1)} %copy.119), kind=kLoop, calls=%fused_computation.4 | loop fusion | flops 5111808 | bytes 2886784 | tf_op jit(solution)/shard_map/reduce_sum | solution.py:147
  (59 shorter events, 0.3 us)
Async XLA Ops:
  7.2 289.0 %copy-start = (bf16[1,384,2048]{2,1,0:T(8,128)(2,1)S(1)}, bf16[1,384,2048]{2,1,0:T(8,128)(2,1)}, u32[]{:S(2)}) copy-start(bf16[1,384,2048]{2,1,0:T(8,128)(2,1)} %param.39) | copy-start | bytes 4718596
  7.2 169.0 %all-gather.2.cloned.1.call-start = ((), (), s32[]{:S(2)}) async-start(), calls=%async_computation.5 | async-start | bytes 17301504 | tf_op jit(solution)/shard_map/all_gather | solution.py:108
  9.3 14.4 %all-to-all-start.1 = ((bf16[64,32,2]{0,2,1:T(2,128)(2,1)}), bf16[64,32,2]{0,2,1:T(2,128)(2,1)S(1)}, u32[]{:S(2)}, u32[]{:S(2)}) async-start(bf16[64,32,2]{0,2,1:T(2,128)(2,1)} %bitcast.14), calls=%async_computation.1 | async-start | bytes 32768 | tf_op jit(solution)/shard_map/all_to_all | solution.py:90
  19.8 7.5 %copy-start.11 = (s32[64,10]{0,1:T(8,128)S(1)}, s32[64,10]{0,1:T(8,128)}, u32[]{:S(2)}) copy-start(s32[64,10]{0,1:T(8,128)} %param.34) | copy-start | bytes 7684
  19.8 7.5 %copy-start.13 = (s32[32]{0:T(128)S(1)}, s32[32]{0:T(128)}, u32[]{:S(2)}) copy-start(s32[32]{0:T(128)} %param.36) | copy-start | bytes 388
  19.8 8.0 %copy-start.16 = (f32[64]{0:T(128)S(1)}, f32[64]{0:T(128)}, u32[]{:S(2)}) copy-start(f32[64]{0:T(128)} %param.26) | copy-start | bytes 772
  19.8 8.1 %copy-start.12 = (f32[64]{0:T(128)S(1)}, f32[64]{0:T(128)}, u32[]{:S(2)}) copy-start(f32[64]{0:T(128)} %param.25) | copy-start | bytes 772
  19.8 8.1 %copy-start.5 = (bf16[64,64]{1,0:T(8,128)(2,1)S(1)}, bf16[64,64]{1,0:T(8,128)(2,1)}, u32[]{:S(2)}) copy-start(bf16[64,64]{1,0:T(8,128)(2,1)} %param.24) | copy-start | bytes 24580
  19.8 8.4 %copy-start.3 = (bf16[64,4096]{1,0:T(8,128)(2,1)S(1)}, bf16[64,4096]{1,0:T(8,128)(2,1)}, u32[]{:S(2)}) copy-start(bf16[64,4096]{1,0:T(8,128)(2,1)} %param.20) | copy-start | bytes 1572868
  23.7 104.2 %all-to-all-start = ((bf16[2,64,64,128]{3,2,0,1:T(8,128)(2,1)}), bf16[2,64,64,128]{3,2,0,1:T(8,128)(2,1)}, u32[]{:S(2)}, u32[]{:S(2)}) async-start(bf16[2,64,64,128]{3,2,0,1:T(8,128)(2,1)} %copy.105), calls=%async_computation | async-start | bytes 4194304 | tf_op jit(solution)/shard_map/all_to_all | solution.py:75
  27.2 2.2 copy-start.6
  27.2 2.1 copy-start.9
  27.2 2.3 copy-start.17
  34.0 3.9 copy-start.18
  143.8 32.2 %copy-start.8 = (f32[4096]{0:T(1024)S(1)}, f32[4096]{0:T(1024)}, u32[]{:S(2)}) copy-start(f32[4096]{0:T(1024)} %param.28) | copy-start | bytes 49156
  143.8 30.7 %all-to-all-start.2 = ((bf16[32,64,128]{2,1,0:T(8,128)(2,1)}), bf16[32,64,128]{2,1,0:T(8,128)(2,1)S(1)}, u32[]{:S(2)}, u32[]{:S(2)}) async-start(bf16[32,64,128]{2,1,0:T(8,128)(2,1)} %all_to_all.45), calls=%async_computation.2 | async-start | bytes 1048576 | tf_op jit(solution)/shard_map/all_to_all | solution.py:93
  163.6 12.6 %copy-start.4 = (bf16[64,2048]{1,0:T(8,128)(2,1)S(1)}, bf16[64,2048]{1,0:T(8,128)(2,1)}, u32[]{:S(2)}) copy-start(bf16[64,2048]{1,0:T(8,128)(2,1)} %param.31) | copy-start | bytes 786436
  176.2 9.1 %copy-start.2 = (bf16[64,4096]{1,0:T(8,128)(2,1)}, bf16[64,4096]{1,0:T(8,128)(2,1)S(1)}, u32[]{:S(2)}) copy-start(bf16[64,4096]{1,0:T(8,128)(2,1)S(1)} %multiply_convert_fusion.3) | copy-start | bytes 1572868
  176.2 9.1 %copy-start.10 = (f32[2048]{0:T(1024)S(1)}, f32[2048]{0:T(1024)}, u32[]{:S(2)}) copy-start(f32[2048]{0:T(1024)} %param.33) | copy-start | bytes 24580
  194.0 98.5 %copy-start.14 = (bf16[1,2048,384]{2,1,0:T(8,128)(2,1)S(1)}, bf16[1,2048,384]{2,1,0:T(8,128)(2,1)}, u32[]{:S(2)}) copy-start(bf16[1,2048,384]{2,1,0:T(8,128)(2,1)} %param.37) | copy-start | bytes 4718596
  290.6 2.0 copy-start.1
  292.6 3.6 copy-start.15
  303.9 4.4 %copy-start.7 = (s32[64,10]{0,1:T(8,128)S(1)}, s32[64,10]{0,1:T(8,128)}, u32[]{:S(2)}) copy-start(s32[64,10]{0,1:T(8,128)} %param.35) | copy-start | bytes 7684
  303.9 97.9 %all-to-all-start.4 = ((bf16[32,32,2048]{2,1,0:T(8,128)(2,1)}), bf16[32,32,2048]{2,1,0:T(8,128)(2,1)}, u32[]{:S(2)}, u32[]{:S(2)}) async-start(bf16[32,32,2048]{2,1,0:T(8,128)(2,1)} %bitcast.88), calls=%async_computation.4 | async-start | bytes 8388608 | tf_op jit(solution)/shard_map/all_to_all | solution.py:143
Sparse Core Ops, SparseCore 0:
  10.9 152.0 all-gather.1
where the time goes:
time: 431 us; the launch traced here: 430 us
  blocking collectives  181 us (42%)
  waiting for transfers between devices  109 us (25%)
  local copies, waits for them, and re-layouts  54.9 us (13%)
  starting transfers between devices  30 us (7%)
  matrix products  26.2 us (6%)
  other arithmetic  15.2 us (4%)
  between operations  14.5 us (3%)
    all_to_all x1, blocking collectives, local(): lax.all_to_all(send_rows, 'wide', split_axis=0, concat_axis=0, tiled=True)  96.5 us
    all_to_all x1, waiting for transfers between devices, local(): lax.all_to_all(outputs, 'wide', split_axis=0, concat_axis=0, tiled=True)  93.3 us
    all_gather x1, blocking collectives, local(): c_all = lax.all_gather(ssd_c, 'wide', axis=0, tiled=True)  84 us
    all_to_all x1, starting transfers between devices, local(): lax.all_to_all(carried_head.reshape(tokens_all, per_dev * head_dim), 'wid...  15.1 us
    gather x2, local copies, waits for them, and re-layouts, local(): jnp.take(returned.reshape(devices * capacity, width), position, axis=0)  15.1 us
    all_to_all x1, waiting for transfers between devices, local(): lax.all_to_all(carried_head.reshape(tokens_all, per_dev * head_dim), 'wid...  10.9 us
    dot_general x1, matrix products, local(): jnp.dot(ssd_out, lax.all_gather(w_out, 'wide', axis=0, tiled=True), prefe...  9.07 us
  transfers between devices with their start and end apart: 5, of which 3 were waited for; matrix products, arithmetic and copies ran while one was open for 9% of the time, Pallas kernels for 0%

commit v1 on v0

--- a/solution.py
+++ b/solution.py
@@ -26,11 +26,12 @@
     return (product * jnp.exp(cumulative)[..., None]).astype(jnp.bfloat16)
 
 
-def expert_mlp(row_set, gate_weight, up_weight, down_weight):
+def expert_mlp(row_set, gate_weight, up_weight, down_weight, share):
     gate_out = jnp.dot(row_set, gate_weight, preferred_element_type=jnp.float32)
     up_out = jnp.dot(row_set, up_weight, preferred_element_type=jnp.float32)
     hidden = (jax.nn.silu(gate_out) * up_out).astype(jnp.bfloat16)
-    return jnp.dot(hidden, down_weight, preferred_element_type=jnp.float32).astype(jnp.bfloat16)
+    result = jnp.dot(hidden, down_weight, preferred_element_type=jnp.float32)
+    return (result * share[:, None]).astype(jnp.bfloat16)
 
 
 def head_steps(raw_steps, bias_part, rate_part, requests):
@@ -108,43 +109,23 @@
         lax.all_gather(w_out, "wide", axis=0, tiled=True),
         preferred_element_type=jnp.float32,
     )
-    topk = expert_ids.shape[1]
-    expert_count = expert_home.shape[0]
     wide_moe = resid.astype(jnp.float32) + projected
     normed = (
         wide_moe
         * lax.rsqrt(jnp.mean(wide_moe * wide_moe, axis=-1, keepdims=True) + 1e-05)
         * moe_gain
     ).astype(jnp.bfloat16)
-    weight_f = route_weight.astype(jnp.float32)
-    share = weight_f / jnp.sum(weight_f, axis=-1, keepdims=True)
-    lookup = expert_ids[..., None] == jnp.arange(expert_count, dtype=jnp.int32)
-    target = jnp.sum(jnp.where(lookup, expert_home, 0), axis=-1)
-    pair_count = tok_dev * topk
-    flat_target = target.reshape(pair_count)
-    one_hot = (flat_target[:, None] == jnp.arange(devices, dtype=jnp.int32)).astype(jnp.int32)
-    before = jnp.cumsum(one_hot, axis=0) - one_hot
-    slot_of = jnp.sum(before * one_hot, axis=-1)
-    capacity = tok_dev * topk // expert_count * 8 // 5
-    position = flat_target * capacity + slot_of
-    source_row = (
-        jnp.zeros((devices * capacity,), jnp.int32)
-        .at[position]
-        .set(jnp.arange(pair_count, dtype=jnp.int32) // topk + 1)
+    tokens = lax.all_gather(normed, "wide", axis=0, tiled=True)
+    routes = lax.all_gather(
+        jnp.concatenate([expert_ids, route_weight], axis=1), "wide", axis=0, tiled=True
     )
-    filled = source_row > 0
-    fetched = jnp.take(normed, jnp.maximum(source_row - 1, 0), axis=0)
-    send_rows = jnp.where(filled[:, None], fetched, jnp.zeros((), jnp.bfloat16)).reshape(
-        devices, capacity, width
-    )
-    received = lax.all_to_all(send_rows, "wide", split_axis=0, concat_axis=0, tiled=True)
-    flat_rows = received.reshape(-1, received.shape[-1])
-    outputs = expert_mlp(flat_rows, w_gate[0], w_up[0], w_down[0]).reshape(received.shape)
-    returned = lax.all_to_all(outputs, "wide", split_axis=0, concat_axis=0, tiled=True)
-    gathered = jnp.take(returned.reshape(devices * capacity, width), position, axis=0).reshape(
-        tok_dev, topk, width
-    )
-    moe_out = jnp.sum(gathered.astype(jnp.float32) * share[..., None], axis=1).astype(jnp.bfloat16)
+    topk = expert_ids.shape[1]
+    ids_all, weight_all = routes[:, :topk], routes[:, topk:].astype(jnp.float32)
+    my_expert = jnp.argmax(expert_home == my_index).astype(jnp.int32)
+    chosen = jnp.sum(jnp.where(ids_all == my_expert, weight_all, 0.0), axis=-1)
+    my_share = chosen / jnp.sum(weight_all, axis=-1)
+    outputs = expert_mlp(tokens, w_gate[0], w_up[0], w_down[0], my_share)
+    moe_out = lax.psum_scatter(outputs, "wide", scatter_dimension=0, tiled=True)
     return (ssd_out, moe_out)
 
 

time: 431 us -> 434 us (level)
  waiting for transfers between devices: 109 us -> 195 us
  blocking collectives: 181 us -> 135 us
  local copies, waits for them, and re-layouts: 54.9 us -> 23.5 us
  other arithmetic: 15.2 us -> 5.36 us
  matrix products: 26.2 us -> 34.5 us
    reduce_scatter x0 -> x1, waiting for transfers between devices: none -> 147 us  [local(): moe_out = lax.psum_scatter(outputs, 'wide', scatter_dimension=0, tiled=True)]
    all_to_all x1 -> x0, blocking collectives: 96.5 us -> none  [local(): lax.all_to_all(send_rows, 'wide', split_axis=0, concat_axis=0, tiled=True)]
    all_to_all x1 -> x0, waiting for transfers between devices: 93.3 us -> none  [local(): lax.all_to_all(outputs, 'wide', split_axis=0, concat_axis=0, tiled=True)]
    all_gather x0 -> x1, blocking collectives: none -> 40.6 us  [local(): lax.all_gather(jnp.concatenate([expert_ids, route_weight], axis=1), 'wide...]
    all_gather x0 -> x1, waiting for transfers between devices: none -> 34.2 us  [local(): tokens = lax.all_gather(normed, 'wide', axis=0, tiled=True)]
    gather x3 -> x0, local copies, waits for them, and re-layouts: 21.1 us -> none  [the longest x2 15.1 us: local(): jnp.take(returned.reshape(devices * capacity, width), position, axis=0)]
    all_gather x1, blocking collectives: 84 us -> 94.5 us  [local(): c_all = lax.all_gather(ssd_c, 'wide', axis=0, tiled=True)]
    reduce_sum x4 -> x1, other arithmetic: 6.65 us -> 0.74 us  [local(): my_share = chosen / jnp.sum(weight_all, axis=-1)]
  transfers between devices with their start and end apart: 5 -> 6, of which waited for: 3 -> 4; matrix products, arithmetic and copies ran while one was open for 9% -> 7% of each run, Pallas kernels for 0% -> 0%
where the time goes in v1:
time: 434 us; the launch traced here: 433 us
  waiting for transfers between devices  195 us (45%)
  blocking collectives  135 us (31%)
  matrix products  34.5 us (8%)
  starting transfers between devices  26 us (6%)
  local copies, waits for them, and re-layouts  23.5 us (5%)
  between operations  14.2 us (3%)
  other arithmetic  5.36 us (1%)
    reduce_scatter x1, waiting for transfers between devices, local(): moe_out = lax.psum_scatter(outputs, 'wide', scatter_dimension=0, tiled=True)  147 us
    all_gather x1, blocking collectives, local(): c_all = lax.all_gather(ssd_c, 'wide', axis=0, tiled=True)  94.5 us
    all_gather x1, blocking collectives, local(): lax.all_gather(jnp.concatenate([expert_ids, route_weight], axis=1), 'wide...  40.6 us
    all_gather x1, waiting for transfers between devices, local(): tokens = lax.all_gather(normed, 'wide', axis=0, tiled=True)  34.2 us
    all_to_all x1, starting transfers between devices, local(): lax.all_to_all(carried_head.reshape(tokens_all, per_dev * head_dim), 'wid...  15 us
    dot_general x1, matrix products, local(): jnp.dot(ssd_out, lax.all_gather(w_out, 'wide', axis=0, tiled=True), prefe...  9.07 us
  transfers between devices with their start and end apart: 6, of which 4 were waited for; matrix products, arithmetic and copies ran while one was open for 7% of the time, Pallas kernels for 0%

profile of v1, /device:TPU:0, one launch (start us, length us, event | category | flops | bytes accessed | tf_op | source)
XLA Modules:
  0.0 433.5 jit_solution(3713584797950371639)
XLA Ops:
  7.2 0.0 copy-start
  7.2 0.0 all-gather.4.cloned.1.call-start
  7.2 0.7 all-gather.4.cloned.1.call-update
  7.9 1.4 copy.78
  9.3 7.3 %all-to-all-start.1 = ((bf16[64,32,2]{0,2,1:T(2,128)(2,1)}), bf16[64,32,2]{0,2,1:T(2,128)(2,1)S(1)}, u32[]{:S(2)}, u32[]{:S(2)}) async-start(bf16[64,32,2]{0,2,1:T(2,128)(2,1)} %bitcast.14), calls=%async_computation.1 | async-start | bytes 32768 | tf_op jit(solution)/shard_map/all_to_all | solution.py:91
  16.6 3.1 copy.75
  19.8 3.9 all-to-all-done.1
  23.7 3.5 all-to-all-start
  27.2 0.1 dynamic_slice.7
  27.3 0.1 dynamic_slice.6
  27.4 94.5 %all_gather.12 = bf16[2048,128]{1,0:T(8,128)(2,1)S(1)} all-gather(bf16[64,128]{1,0:T(8,128)(2,1)S(1)} %copy-done.4), channel_id=1, replica_groups=mesh['group'=1,'wide'=32] {'wide'}, dimensions={0}, use_global_device_ids=true | all-gather | bytes 540672 | tf_op jit(solution)/shard_map/all_gather | solution.py:90
  121.9 0.1 reshape.105
  122.0 0.1 copy.80
  122.1 0.1 fusion.25
  122.2 0.4 copy.81
  122.6 1.1 reduce-window_exponential_fusion
  123.7 1.8 copy.82
  125.5 0.0 all-to-all-done
  125.5 3.2 copy.77
  128.7 3.7 gather_fusion
  132.5 3.7 fusion
  136.2 0.0 copy-start.3
  136.2 1.1 copy.83
  137.3 0.0 copy-start.6
  137.3 0.0 copy-start.16
  137.3 1.3 all_to_all.39
  138.6 15.0 %all-to-all-start.2 = ((bf16[32,64,128]{2,1,0:T(8,128)(2,1)}), bf16[32,64,128]{2,1,0:T(8,128)(2,1)S(1)}, u32[]{:S(2)}, u32[]{:S(2)}) async-start(bf16[32,64,128]{2,1,0:T(8,128)(2,1)} %all_to_all.39), calls=%async_computation.2 | async-start | bytes 1048576 | tf_op jit(solution)/shard_map/all_to_all | solution.py:94
  153.6 0.2 all-gather.6.cloned.1.call-start
  153.8 0.1 reduce_window_sum.22
  153.9 0.1 copy.69
  154.0 0.1 copy.71
  154.1 2.1 reshape.102
  156.2 0.1 fusion.29
  156.3 1.9 fusion.9
  158.2 2.5 copy.74
  160.8 2.1 reshape.104
  162.9 0.0 copy-start.5
  162.9 0.0 copy-start.2
  162.9 8.6 %all-to-all-done.2 = bf16[32,64,128]{2,1,0:T(8,128)(2,1)S(1)} async-done(((bf16[32,64,128]{2,1,0:T(8,128)(2,1)}), bf16[32,64,128]{2,1,0:T(8,128)(2,1)S(1)}, u32[]{:S(2)}, u32[]{:S(2)}) %all-to-all-start.2) | async-done | bytes 524320 | tf_op jit(solution)/shard_map/all_to_all | solution.py:94
  171.5 1.5 multiply_reduce_fusion
  173.1 0.2 multiply_convert_fusion.4
  173.3 0.0 copy-start.1
  173.3 0.0 copy-start.7
  173.3 0.0 copy-start.8
  173.3 0.0 copy-start.9
  173.3 0.0 all-gather.4.cloned.1.call-done
  173.3 0.0 copy-done.2
  173.3 9.1 %multiply_reduce_fusion.1 = (f32[64]{0:T(128)S(1)}, f32[64,2048]{1,0:T(8,128)S(1)}) fusion(bf16[64,4096]{1,0:T(8,128)(2,1)S(1)} %multiply_convert_fusion.4, bf16[4096,2048]{1,0:T(8,128)(2,1)} %all-gather.4.cloned.1.call-done, bf16[64,2048]{1,0:T(8,128)(2,1)S(1)} %copy-done.2), kind=kOutput, calls=%fused_computation.36 | convolution fusion | flops 1074266112 | bytes 18088192 | tf_op jit(solution)/shard_map/dot_general | solution.py:107
  182.4 0.0 copy-start.11
  182.5 0.8 multiply_convert_fusion.5
  183.3 0.0 all-gather.6.cloned.1.call-update
  183.3 0.0 reduce-scatter.2.cloned.1.call-start
  183.4 40.6 %all-gather = s32[32,64,20]{1,2,0:T(8,128)S(1)} all-gather(s32[1,64,20]{1,2,0:T(8,128)S(1)} %add_bitcast_fusion), channel_id=1, replica_groups=mesh['group'=1,'wide'=32] {'wide'}, dimensions={0}, use_global_device_ids=true | all-gather | bytes 168960 | tf_op jit(solution)/shard_map/all_gather | solution.py:119
  224.0 0.1 copy.85
  224.1 0.1 reshape.117
  224.2 0.7 compare_reduce_fusion
  224.9 0.7 fusion.24
  225.7 0.0 copy-start.13
  225.7 34.2 %all-gather.6.cloned.1.call-done = bf16[2048,2048]{1,0:T(8,128)(2,1)} async-done(((bf16[64,2048]{1,0:T(8,128)(2,1)}), bf16[2048,2048]{1,0:T(8,128)(2,1)}) %all-gather.6.cloned.1.call-update) | async-done | bytes 8388624 | tf_op jit(solution)/shard_map/all_gather | solution.py:118
  259.9 7.7 %fusion.7 = f32[2048,384]{1,0:T(8,128)S(1)} fusion(bf16[2048,2048]{1,0:T(8,128)(2,1)} %all-gather.6.cloned.1.call-done, bf16[1,2048,384]{2,1,0:T(8,128)(2,1)} %param.37), kind=kOutput, calls=%fused_computation.14 | convolution fusion | flops 3221225472 | bytes 13107200 | tf_op jit(solution)/shard_map/dot_general | solution.py:30
  267.6 5.2 %multiply_convert_fusion.1 = bf16[2048,384]{1,0:T(8,128)(2,1)S(1)} fusion(f32[2048,384]{1,0:T(8,128)S(1)} %fusion.7, bf16[2048,2048]{1,0:T(8,128)(2,1)S(1)} %copy-done.12, bf16[1,2048,384]{2,1,0:T(8,128)(2,1)S(1)} %copy-done.13), kind=kOutput, calls=%fused_computation.2 | convolution fusion | flops 3225944064 | bytes 14680064 | tf_op jit(solution)/shard_map/dot_general | solution.py:31
  272.8 6.8 %multiply_convert_fusion = bf16[2048,2048]{1,0:T(8,128)(2,1)} fusion(bf16[2048,384]{1,0:T(8,128)(2,1)S(1)} %multiply_convert_fusion.1, f32[2048]{0:T(1024)S(1)} %div.33, bf16[1,384,2048]{2,1,0:T(8,128)(2,1)S(1)} %copy-done), kind=kOutput, calls=%fused_computation.1 | convolution fusion | flops 3229614080 | bytes 11542528 | tf_op jit(solution)/shard_map/dot_general | solution.py:33
  279.6 0.0 reduce-scatter.2.cloned.1.call-update
  279.6 147.3 %reduce-scatter.2.cloned.1.call-done = bf16[64,2048]{1,0:T(8,128)(2,1)} async-done(((bf16[2048,2048]{1,0:T(8,128)(2,1)}), bf16[64,2048]{1,0:T(8,128)(2,1)}) %reduce-scatter.2.cloned.1.call-update) | async-done | bytes 262160 | tf_op jit(solution)/shard_map/reduce_scatter | solution.py:128
  (34 shorter events, 0.2 us)
Async XLA Ops:
  7.2 265.6 %copy-start = (bf16[1,384,2048]{2,1,0:T(8,128)(2,1)S(1)}, bf16[1,384,2048]{2,1,0:T(8,128)(2,1)}, u32[]{:S(2)}) copy-start(bf16[1,384,2048]{2,1,0:T(8,128)(2,1)} %param.39) | copy-start | bytes 4718596
  7.2 166.1 %all-gather.4.cloned.1.call-start = ((), (), s32[]{:S(2)}) async-start(), calls=%async_computation.4 | async-start | bytes 17301504 | tf_op jit(solution)/shard_map/all_gather | solution.py:109
  9.3 14.4 %all-to-all-start.1 = ((bf16[64,32,2]{0,2,1:T(2,128)(2,1)}), bf16[64,32,2]{0,2,1:T(2,128)(2,1)S(1)}, u32[]{:S(2)}, u32[]{:S(2)}) async-start(bf16[64,32,2]{0,2,1:T(2,128)(2,1)} %bitcast.14), calls=%async_computation.1 | async-start | bytes 32768 | tf_op jit(solution)/shard_map/all_to_all | solution.py:91
  19.8 7.4 %copy-start.14 = (f32[64]{0:T(128)S(1)}, f32[64]{0:T(128)}, u32[]{:S(2)}) copy-start(f32[64]{0:T(128)} %param.26) | copy-start | bytes 772
  19.8 7.5 %copy-start.10 = (f32[64]{0:T(128)S(1)}, f32[64]{0:T(128)}, u32[]{:S(2)}) copy-start(f32[64]{0:T(128)} %param.25) | copy-start | bytes 772
  19.8 7.6 %copy-start.15 = (s32[64]{0:T(128)S(1)}, s32[64]{0:T(128)}, u32[]{:S(2)}) copy-start(s32[64]{0:T(128)} %param.30) | copy-start | bytes 772
  19.8 7.6 %copy-start.4 = (bf16[64,128]{1,0:T(8,128)(2,1)S(1)}, bf16[64,128]{1,0:T(8,128)(2,1)}, u32[]{:S(2)}) copy-start(bf16[64,128]{1,0:T(8,128)(2,1)} %param.23) | copy-start | bytes 49156
  23.7 101.8 %all-to-all-start = ((bf16[2,64,64,128]{3,2,0,1:T(8,128)(2,1)}), bf16[2,64,64,128]{3,2,0,1:T(8,128)(2,1)}, u32[]{:S(2)}, u32[]{:S(2)}) async-start(bf16[2,64,64,128]{3,2,0,1:T(8,128)(2,1)} %copy.75), calls=%async_computation | async-start | bytes 4194304 | tf_op jit(solution)/shard_map/all_to_all | solution.py:76
  136.2 17.6 %copy-start.3 = (bf16[64,64]{1,0:T(8,128)(2,1)S(1)}, bf16[64,64]{1,0:T(8,128)(2,1)}, u32[]{:S(2)}) copy-start(bf16[64,64]{1,0:T(8,128)(2,1)} %param.24) | copy-start | bytes 24580
  137.3 18.9 %copy-start.6 = (bf16[64,128]{1,0:T(8,128)(2,1)S(1)}, bf16[64,128]{1,0:T(8,128)(2,1)}, u32[]{:S(2)}) copy-start(bf16[64,128]{1,0:T(8,128)(2,1)} %param.22) | copy-start | bytes 49156
  137.3 19.0 %copy-start.16 = (f32[64]{0:T(128)S(1)}, f32[64]{0:T(128)}, u32[]{:S(2)}) copy-start(f32[64]{0:T(128)} %param.27) | copy-start | bytes 772
  138.6 32.9 %all-to-all-start.2 = ((bf16[32,64,128]{2,1,0:T(8,128)(2,1)}), bf16[32,64,128]{2,1,0:T(8,128)(2,1)S(1)}, u32[]{:S(2)}, u32[]{:S(2)}) async-start(bf16[32,64,128]{2,1,0:T(8,128)(2,1)} %all_to_all.39), calls=%async_computation.2 | async-start | bytes 1048576 | tf_op jit(solution)/shard_map/all_to_all | solution.py:94
  153.6 106.3 %all-gather.6.cloned.1.call-start = ((), (), s32[]{:S(2)}) async-start(), calls=%async_computation.5 | async-start | bytes 8650752 | tf_op jit(solution)/shard_map/all_gather | solution.py:118
  162.9 10.1 %copy-start.5 = (f32[4096]{0:T(1024)S(1)}, f32[4096]{0:T(1024)}, u32[]{:S(2)}) copy-start(f32[4096]{0:T(1024)} %param.28) | copy-start | bytes 49156
  162.9 10.4 %copy-start.2 = (bf16[64,2048]{1,0:T(8,128)(2,1)S(1)}, bf16[64,2048]{1,0:T(8,128)(2,1)}, u32[]{:S(2)}) copy-start(bf16[64,2048]{1,0:T(8,128)(2,1)} %param.31) | copy-start | bytes 786436
  173.3 9.2 %copy-start.1 = (bf16[64,4096]{1,0:T(8,128)(2,1)}, bf16[64,4096]{1,0:T(8,128)(2,1)S(1)}, u32[]{:S(2)}) copy-start(bf16[64,4096]{1,0:T(8,128)(2,1)S(1)} %multiply_convert_fusion.4) | copy-start | bytes 1572868
  173.3 9.2 %copy-start.7 = (f32[2048]{0:T(1024)S(1)}, f32[2048]{0:T(1024)}, u32[]{:S(2)}) copy-start(f32[2048]{0:T(1024)} %param.33) | copy-start | bytes 24580
  173.3 10.1 %copy-start.8 = (s32[64,10]{0,1:T(8,128)S(1)}, s32[64,10]{0,1:T(8,128)}, u32[]{:S(2)}) copy-start(s32[64,10]{0,1:T(8,128)} %param.35) | copy-start | bytes 7684
  173.3 10.1 %copy-start.9 = (s32[64,10]{0,1:T(8,128)S(1)}, s32[64,10]{0,1:T(8,128)}, u32[]{:S(2)}) copy-start(s32[64,10]{0,1:T(8,128)} %param.34) | copy-start | bytes 7684
  182.4 41.8 %copy-start.11 = (s32[32]{0:T(128)S(1)}, s32[32]{0:T(128)}, u32[]{:S(2)}) copy-start(s32[32]{0:T(128)} %param.36) | copy-start | bytes 388
  183.3 243.6 %reduce-scatter.2.cloned.1.call-start = ((), (), s32[]{:S(2)}) async-start(), calls=%async_computation.6 | async-start | bytes 8650752 | tf_op jit(solution)/shard_map/reduce_scatter | solution.py:128
  225.7 41.9 %copy-start.13 = (bf16[1,2048,384]{2,1,0:T(8,128)(2,1)S(1)}, bf16[1,2048,384]{2,1,0:T(8,128)(2,1)}, u32[]{:S(2)}) copy-start(bf16[1,2048,384]{2,1,0:T(8,128)(2,1)} %param.38) | copy-start | bytes 4718596
  259.9 7.7 %copy-start.12 = (bf16[2048,2048]{1,0:T(8,128)(2,1)S(1)}, bf16[2048,2048]{1,0:T(8,128)(2,1)}, u32[]{:S(2)}) copy-start(bf16[2048,2048]{1,0:T(8,128)(2,1)} %all-gather.6.cloned.1.call-done) | copy-start | bytes 25165828
Sparse Core Ops, SparseCore 0:
  10.9 157.8 all-gather.3
  183.4 76.3 all-gather.5
  279.7 147.1 reduce-scatter.1

commit v2 on v1

--- a/solution.py
+++ b/solution.py
@@ -1,9 +1,15 @@
+import functools
+
 import jax
 import jax.numpy as jnp
 from jax import lax
+from jax.experimental import pallas as pl
+from jax.experimental.pallas import tpu as pltpu
 from jax.sharding import PartitionSpec as P
 
 SEQ = 32
+LANES = 128
+MESH = pl.DeviceIdType.MESH
 
 
 def intra_terms(inputs, step_size, cumulative, b_proj, c_proj, skip_gain):
@@ -26,12 +32,210 @@
     return (product * jnp.exp(cumulative)[..., None]).astype(jnp.bfloat16)
 
 
-def expert_mlp(row_set, gate_weight, up_weight, down_weight, share):
-    gate_out = jnp.dot(row_set, gate_weight, preferred_element_type=jnp.float32)
-    up_out = jnp.dot(row_set, up_weight, preferred_element_type=jnp.float32)
-    hidden = (jax.nn.silu(gate_out) * up_out).astype(jnp.bfloat16)
-    result = jnp.dot(hidden, down_weight, preferred_element_type=jnp.float32)
-    return (result * share[:, None]).astype(jnp.bfloat16)
+def place(devices):
+    me = lax.axis_index("wide")
+    return me // 8, me // 4 % 2, me // 2 % 2, me % 2
+
+
+def expert_kernel(
+    planes,
+    devices,
+    rows_ref,
+    gate_hbm,
+    up_hbm,
+    down_hbm,
+    out_ref,
+    tok,
+    res,
+    from_core,
+    from_a1,
+    from_b1,
+    from_a2,
+    from_b2,
+    from_z,
+    w_in,
+    w_down,
+    local_sem,
+    send_sem,
+    recv_sem,
+):
+    z, y, x, c = place(devices)
+    me = lax.axis_index("wide")
+    half = rows_ref.shape[0] // 2
+    width = down_hbm.shape[1]
+    hid = down_hbm.shape[0]
+    low, high = pl.ds(0, half), pl.ds(half, half)
+
+    def at(zz, yy, xx, cc):
+        return {"wide": ((zz * 2 + yy) * 2 + xx) * 2 + cc}
+
+    to_x, to_y, to_c = at(z, y, 1 - x, c), at(z, 1 - y, x, c), at(z, y, x, 1 - c)
+    others = [at(lax.rem(z + k, planes), y, x, c) for k in range(1, planes)]
+    loads = [
+        pltpu.make_async_copy(gate_hbm, w_in.at[:, pl.ds(0, hid)], local_sem.at[0]),
+        pltpu.make_async_copy(up_hbm, w_in.at[:, pl.ds(hid, hid)], local_sem.at[1]),
+        pltpu.make_async_copy(down_hbm, w_down, local_sem.at[2]),
+    ]
+    for load in loads:
+        load.start()
+    tok[z, c, y, x] = rows_ref[...]
+
+    barrier = pltpu.get_barrier_semaphore()
+    for peer in [to_x, to_y, to_c] + others:
+        pl.semaphore_signal(barrier, inc=1, device_id=peer, device_id_type=MESH)
+    pl.semaphore_wait(barrier, planes + 2)
+
+    started = []
+
+    def send(src, dst, kind, out_slot, in_slot, peer):
+        copy = pltpu.make_async_remote_copy(
+            src_ref=src,
+            dst_ref=dst,
+            send_sem=send_sem.at[kind, out_slot],
+            recv_sem=recv_sem.at[kind, in_slot],
+            device_id=peer,
+            device_id_type=MESH,
+        )
+        copy.start()
+        started.append(copy)
+        return copy
+
+    def arrived(ref, kind, slot):
+        pltpu.make_async_copy(ref, ref, recv_sem.at[kind, slot]).wait()
+
+    for k in range(planes - 1, 0, -1):
+        mine = tok.at[z, c, y, x]
+        send(mine, mine, 0, k, planes - k, others[k - 1])
+
+    def group(j):
+        return lax.rem(z + j, planes)
+
+    def spread_1(j):
+        q = group(j)
+        if j:
+            arrived(tok.at[q, c, y, x], 0, j)
+        part = tok.at[q, c, y, x, low]
+        send(part, part, 1, j, j, to_x)
+        part = tok.at[q, c, y, x, high]
+        send(part, part, 2, j, j, to_y)
+
+    def spread_2(j):
+        q = group(j)
+        arrived(tok.at[q, c, y, 1 - x, low], 1, j)
+        part = tok.at[q, c, y, :, low]
+        send(part, part, 3, j, j, to_y)
+        arrived(tok.at[q, c, 1 - y, x, high], 2, j)
+        part = tok.at[q, c, :, x, high]
+        send(part, part, 4, j, j, to_x)
+
+    def expert(q, side):
+        block = tok[q, side].reshape(8 * half, tok.shape[-1])
+        both = jnp.dot(block[:, :width], w_in[...], preferred_element_type=jnp.float32)
+        hidden = (jax.nn.silu(both[:, :hid]) * both[:, hid:]).astype(jnp.bfloat16)
+        lane = lax.broadcasted_iota(jnp.int32, (1, tok.shape[-1] - width), 1)
+        mine = (lane == me) | (lane == me + devices)
+        share = jnp.sum(
+            jnp.where(mine, block[:, width:].astype(jnp.float32), 0.0), axis=1, keepdims=True
+        )
+        result = jnp.dot(hidden, w_down[...], preferred_element_type=jnp.float32) * share
+        res[q, side] = result.astype(jnp.bfloat16).reshape(2, 2, 2 * half, width)
+
+    def spread_3(j):
+        q = group(j)
+        arrived(tok.at[q, c, 1 - y, :, low], 3, j)
+        arrived(tok.at[q, c, :, 1 - x, high], 4, j)
+        part = tok.at[q, c]
+        send(part, part, 5, j, j, to_c)
+        if j == 0:
+            for load in loads:
+                load.wait()
+        expert(q, c)
+
+    def run(j):
+        q = group(j)
+        arrived(tok.at[q, 1 - c], 5, j)
+        expert(q, 1 - c)
+        send(res.at[q, 1 - c], from_core.at[j], 6, j, j, to_c)
+
+    def plus(a, b):
+        return (a.astype(jnp.float32) + b.astype(jnp.float32)).astype(jnp.bfloat16)
+
+    def sum_1(j):
+        q = group(j)
+        arrived(from_core.at[j], 6, j)
+        res[q, c] = plus(res[q, c], from_core[j])
+        send(res.at[q, c, 1 - y, :, low], from_a1.at[j], 7, j, j, to_y)
+        send(res.at[q, c, :, 1 - x, high], from_b1.at[j], 8, j, j, to_x)
+
+    def sum_2(j):
+        q = group(j)
+        arrived(from_a1.at[j], 7, j)
+        res[q, c, y, :, low] = plus(res[q, c, y, :, low], from_a1[j])
+        send(res.at[q, c, y, 1 - x, low], from_a2.at[j], 9, j, j, to_x)
+        arrived(from_b1.at[j], 8, j)
+        res[q, c, :, x, high] = plus(res[q, c, :, x, high], from_b1[j])
+        send(res.at[q, c, 1 - y, x, high], from_b2.at[j], 10, j, j, to_y)
+
+    def sum_3(j):
+        q = group(j)
+        arrived(from_a2.at[j], 9, j)
+        res[q, c, y, x, low] = plus(res[q, c, y, x, low], from_a2[j])
+        arrived(from_b2.at[j], 10, j)
+        res[q, c, y, x, high] = plus(res[q, c, y, x, high], from_b2[j])
+        if j:
+            send(res.at[q, c, y, x], from_z.at[planes - j], 11, j, planes - j, others[j - 1])
+
+    stages = [spread_1, spread_2, spread_3, run, sum_1, sum_2, sum_3]
+    for tick in range(planes + len(stages) - 1):
+        for number in reversed(range(len(stages))):
+            if 0 <= tick - number < planes:
+                stages[number](tick - number)
+
+    total = res[z, c, y, x].astype(jnp.float32)
+    for j in range(1, planes):
+        arrived(from_z.at[j], 11, j)
+        total = total + from_z[j].astype(jnp.float32)
+    out_ref[...] = total.astype(out_ref.dtype)
+    for copy in started:
+        copy.wait_send()
+
+
+def expert_block(rows, gate_weight, up_weight, down_weight, devices):
+    planes = devices // 8
+    count, wide = rows.shape
+    hid, width = down_weight.shape
+    half = count // 2
+
+    def held(*shape):
+        return pltpu.VMEM(shape, jnp.bfloat16)
+
+    vmem = pl.BlockSpec(memory_space=pltpu.VMEM)
+    hbm = pl.BlockSpec(memory_space=pl.ANY)
+    return pl.pallas_call(
+        functools.partial(expert_kernel, planes, devices),
+        out_shape=jax.ShapeDtypeStruct((count, width), jnp.bfloat16),
+        in_specs=[vmem, hbm, hbm, hbm],
+        out_specs=vmem,
+        scratch_shapes=[
+            held(planes, 2, 2, 2, count, wide),
+            held(planes, 2, 2, 2, count, width),
+            held(planes, 2, 2, count, width),
+            held(planes, 2, half, width),
+            held(planes, 2, half, width),
+            held(planes, half, width),
+            held(planes, half, width),
+            held(planes, count, width),
+            held(width, 2 * hid),
+            held(hid, width),
+            pltpu.SemaphoreType.DMA((3,)),
+            pltpu.SemaphoreType.DMA((12, planes)),
+            pltpu.SemaphoreType.DMA((12, planes)),
+        ],
+        compiler_params=pltpu.CompilerParams(
+            collective_id=0, has_side_effects=True, vmem_limit_bytes=60 * 1024 * 1024
+        ),
+        name="expert_block",
+    )(rows, gate_weight, up_weight, down_weight)
 
 
 def head_steps(raw_steps, bias_part, rate_part, requests):
@@ -115,17 +319,19 @@
         * lax.rsqrt(jnp.mean(wide_moe * wide_moe, axis=-1, keepdims=True) + 1e-05)
         * moe_gain
     ).astype(jnp.bfloat16)
-    tokens = lax.all_gather(normed, "wide", axis=0, tiled=True)
-    routes = lax.all_gather(
-        jnp.concatenate([expert_ids, route_weight], axis=1), "wide", axis=0, tiled=True
-    )
-    topk = expert_ids.shape[1]
-    ids_all, weight_all = routes[:, :topk], routes[:, topk:].astype(jnp.float32)
-    my_expert = jnp.argmax(expert_home == my_index).astype(jnp.int32)
-    chosen = jnp.sum(jnp.where(ids_all == my_expert, weight_all, 0.0), axis=-1)
-    my_share = chosen / jnp.sum(weight_all, axis=-1)
-    outputs = expert_mlp(tokens, w_gate[0], w_up[0], w_down[0], my_share)
-    moe_out = lax.psum_scatter(outputs, "wide", scatter_dimension=0, tiled=True)
+    weight_f = route_weight.astype(jnp.float32)
+    share = weight_f / jnp.sum(weight_f, axis=-1, keepdims=True)
+    lookup = expert_ids[..., None] == jnp.arange(expert_home.shape[0], dtype=jnp.int32)
+    target = jnp.sum(jnp.where(lookup, expert_home, 0), axis=-1)
+    spread = jnp.sum(
+        jnp.where(target[..., None] == jnp.arange(devices, dtype=jnp.int32), share[..., None], 0.0),
+        axis=1,
+    )
+    high = spread.astype(jnp.bfloat16)
+    low = (spread - high.astype(jnp.float32)).astype(jnp.bfloat16)
+    pad = jnp.zeros((tok_dev, -(2 * devices) % LANES), jnp.bfloat16)
+    rows = jnp.concatenate([normed, high, low, pad], axis=1)
+    moe_out = expert_block(rows, w_gate[0], w_up[0], w_down[0], devices)
     return (ssd_out, moe_out)
 
 

time: 434 us -> 289 us (0.67)
  waiting for transfers between devices: 195 us -> 16.3 us
  Pallas kernels: 0 us -> 95.8 us
  blocking collectives: 135 us -> 96.1 us
  matrix products: 34.5 us -> 13.5 us
    reduce_scatter x1 -> x0, waiting for transfers between devices: 147 us -> none  [local(): moe_out = lax.psum_scatter(outputs, 'wide', scatter_dimension=0, tiled=True)]
    pallas_call x0 -> x1, Pallas kernels: none -> 95.8 us  [expert_block(): pl.pallas_call(functools.partial(expert_kernel, planes, devices), out_sha...]
    all_gather x1 -> x0, blocking collectives: 40.6 us -> none  [local(): lax.all_gather(jnp.concatenate([expert_ids, route_weight], axis=1), 'wide...]
    all_gather x1 -> x0, waiting for transfers between devices: 34.2 us -> none  [local(): tokens = lax.all_gather(normed, 'wide', axis=0, tiled=True)]
    dot_general x3 -> x0, matrix products: 19.7 us -> none  [the longest x1 7.7 us: expert_mlp(): gate_out = jnp.dot(row_set, gate_weight, preferred_element_type=jnp.float32)]
  transfers between devices with their start and end apart: 6 -> 4, of which waited for: 4 -> 2; matrix products, arithmetic and copies ran while one was open for 7% -> 8% of each run, Pallas kernels for 0% -> 0%
where the time goes in v2:
time: 289 us; the launch traced here: 288 us
  blocking collectives  96.1 us (33%)
  Pallas kernels  95.8 us (33%)
  starting transfers between devices  29 us (10%)
  local copies, waits for them, and re-layouts  19.6 us (7%)
  waiting for transfers between devices  16.3 us (6%)
  between operations  14.4 us (5%)
  matrix products  13.5 us (5%)
  other arithmetic  3.55 us (1%)
    all_gather x1, blocking collectives, local(): c_all = lax.all_gather(ssd_c, 'wide', axis=0, tiled=True)  96.1 us
    pallas_call x1, Pallas kernels, expert_block(): pl.pallas_call(functools.partial(expert_kernel, planes, devices), out_sha...  95.8 us
    all_to_all x1, starting transfers between devices, local(): lax.all_to_all(carried_head.reshape(tokens_all, per_dev * head_dim), 'wid...  19 us
    all_to_all x1, waiting for transfers between devices, local(): lax.all_to_all(carried_head.reshape(tokens_all, per_dev * head_dim), 'wid...  11.8 us
    dot_general x1, matrix products, local(): jnp.dot(ssd_out, lax.all_gather(w_out, 'wide', axis=0, tiled=True), prefe...  9.07 us
    all_to_all x1, starting transfers between devices, local(): lax.all_to_all(dt_raw, 'wide', split_axis=1, concat_axis=0, tiled=True)  7.3 us
    unnamed x35, local copies, waits for them, and re-layouts  6.36 us
  transfers between devices with their start and end apart: 4, of which 2 were waited for; matrix products, arithmetic and copies ran while one was open for 8% of the time, Pallas kernels for 0%

profile of v2, /device:TPU:0, one launch (start us, length us, event | category | flops | bytes accessed | tf_op | source)
XLA Modules:
  0.0 288.3 jit_solution(9906620120249640856)
XLA Ops:
  7.2 0.0 copy-start
  7.2 0.0 all-gather.2.cloned.1.call-start
  7.2 0.7 all-gather.2.cloned.1.call-update
  7.9 1.4 copy.100
  9.3 7.3 %all-to-all-start.1 = ((bf16[64,32,2]{0,2,1:T(2,128)(2,1)}), bf16[64,32,2]{0,2,1:T(2,128)(2,1)S(1)}, u32[]{:S(2)}, u32[]{:S(2)}) async-start(bf16[64,32,2]{0,2,1:T(2,128)(2,1)} %bitcast.14), calls=%async_computation.1 | async-start | bytes 32768 | tf_op jit(solution)/shard_map/all_to_all | solution.py:295
  16.6 3.2 %copy.97 = bf16[2,64,64,128]{3,2,0,1:T(8,128)(2,1)} copy(bf16[2,64,64,128]{3,2,1,0:T(8,128)(2,1)} %param.29) | data formatting | bytes 4194304 | tf_op args[9]
  19.8 0.0 copy-start.11
  19.8 0.0 copy-start.14
  19.9 0.0 copy-start.5
  19.9 0.0 copy-start.6
  19.9 3.8 %all-to-all-done.1 = bf16[64,32,2]{0,2,1:T(2,128)(2,1)S(1)} async-done(((bf16[64,32,2]{0,2,1:T(2,128)(2,1)}), bf16[64,32,2]{0,2,1:T(2,128)(2,1)S(1)}, u32[]{:S(2)}, u32[]{:S(2)}) %all-to-all-start.1) | async-done | bytes 8224 | tf_op jit(solution)/shard_map/all_to_all | solution.py:295
  23.7 2.7 all-to-all-start
  26.4 0.0 copy-done.7
  26.5 0.0 copy-done.10
  26.5 0.0 copy-done.12
  26.5 0.1 select_reduce_fusion.1
  26.7 0.1 copy.108
  26.7 0.0 copy-done.13
  26.8 0.1 dynamic_slice.7
  26.8 0.0 copy-done.11
  26.8 0.1 dynamic_slice.6
  26.9 0.0 copy-done.14
  26.9 0.0 copy-done.5
  27.0 0.0 copy-done.6
  27.0 96.1 %all_gather.6 = bf16[2048,128]{1,0:T(8,128)(2,1)} all-gather(bf16[64,128]{1,0:T(8,128)(2,1)S(1)} %copy-done.6), channel_id=1, replica_groups=mesh['group'=1,'wide'=32] {'wide'}, dimensions={0}, use_global_device_ids=true | all-gather | bytes 540672 | tf_op jit(solution)/shard_map/all_gather | solution.py:294
  123.1 0.1 reshape.104
  123.2 0.1 copy.102
  123.3 0.1 fusion.20
  123.4 0.4 copy.103
  123.8 1.2 reduce-window_exponential_fusion
  125.0 1.8 copy.104
  126.8 0.0 all-to-all-done
  126.8 1.6 copy.99
  128.4 2.6 gather_fusion
  131.0 0.0 copy-done.3
  131.0 2.3 fusion
  133.4 0.0 copy-start.2
  133.4 1.1 copy.105
  134.5 0.0 copy-start.15
  134.5 1.3 all_to_all.39
  135.8 19.0 %all-to-all-start.2 = ((bf16[32,64,128]{2,1,0:T(8,128)(2,1)}), bf16[32,64,128]{2,1,0:T(8,128)(2,1)}, u32[]{:S(2)}, u32[]{:S(2)}) async-start(bf16[32,64,128]{2,1,0:T(8,128)(2,1)} %all_to_all.39), calls=%async_computation.2 | async-start | bytes 1048576 | tf_op jit(solution)/shard_map/all_to_all | solution.py:298
  154.8 0.1 reduce_window_sum.22
  154.8 0.1 copy.91
  154.9 0.1 copy.93
  155.0 0.0 copy-done.2
  155.0 1.1 reshape.101
  156.2 0.1 fusion.24
  156.3 1.9 fusion.5
  158.2 1.2 copy.96
  159.5 0.7 reshape.103
  160.1 0.0 copy-start.8
  160.1 0.1 copy.109
  160.2 0.0 copy-start.4
  160.2 11.8 %all-to-all-done.2 = bf16[32,64,128]{2,1,0:T(8,128)(2,1)} async-done(((bf16[32,64,128]{2,1,0:T(8,128)(2,1)}), bf16[32,64,128]{2,1,0:T(8,128)(2,1)}, u32[]{:S(2)}, u32[]{:S(2)}) %all-to-all-start.2) | async-done | bytes 524320 | tf_op jit(solution)/shard_map/all_to_all | solution.py:298
  172.0 1.7 multiply_reduce_fusion
  173.7 0.2 multiply_convert_fusion.2
  173.9 0.0 copy-start.1
  173.9 0.0 copy-start.9
  173.9 0.0 all-gather.2.cloned.1.call-done
  174.0 9.1 %multiply_reduce_fusion.1 = (f32[64]{0:T(128)S(1)}, f32[64,2048]{1,0:T(8,128)S(1)}) fusion(bf16[64,4096]{1,0:T(8,128)(2,1)S(1)} %multiply_convert_fusion.2, bf16[4096,2048]{1,0:T(8,128)(2,1)} %all-gather.2.cloned.1.call-done, bf16[64,2048]{1,0:T(8,128)(2,1)S(1)} %copy-done.4), kind=kOutput, calls=%fused_computation.30 | convolution fusion | flops 1074266112 | bytes 18088192 | tf_op jit(solution)/shard_map/dot_general | solution.py:311
  183.1 0.1 multiply_convert_fusion.3
  183.2 0.8 concatenate.3.rows_ref
  184.0 95.8 %expert_block.1 = bf16[64,2048]{1,0:T(8,128)(2,1)} custom-call(bf16[64,2176]{1,0:T(8,128)(2,1)} %concatenate.3.rows_ref, bf16[2048,384]{1,0:T(8,128)(2,1)} %bitcast.53, bf16[2048,384]{1,0:T(8,128)(2,1)} %bitcast.54, bf16[384,2048]{1,0:T(8,128)(2,1)} %bitcast.55), custom_call_target="tpu_custom_call" | custom-call | tf_op jit(solution)/shard_map/expert_block/pallas_call | solution.py:214
  279.8 1.7 copy.118
  (28 shorter events, 0.2 us)
Async XLA Ops:
  7.2 149.0 %copy-start = (bf16[64,128]{1,0:T(8,128)(2,1)S(1)}, bf16[64,128]{1,0:T(8,128)(2,1)}, u32[]{:S(2)}) copy-start(bf16[64,128]{1,0:T(8,128)(2,1)} %param.22) | copy-start | bytes 49156
  7.2 166.8 %all-gather.2.cloned.1.call-start = ((), (), s32[]{:S(2)}) async-start(), calls=%async_computation.3 | async-start | bytes 17301504 | tf_op jit(solution)/shard_map/all_gather | solution.py:313
  9.3 14.4 %all-to-all-start.1 = ((bf16[64,32,2]{0,2,1:T(2,128)(2,1)}), bf16[64,32,2]{0,2,1:T(2,128)(2,1)S(1)}, u32[]{:S(2)}, u32[]{:S(2)}) async-start(bf16[64,32,2]{0,2,1:T(2,128)(2,1)} %bitcast.14), calls=%async_computation.1 | async-start | bytes 32768 | tf_op jit(solution)/shard_map/all_to_all | solution.py:295
  19.8 6.6 %copy-start.7 = (s32[64,10]{0,1:T(8,128)S(1)}, s32[64,10]{0,1:T(8,128)}, u32[]{:S(2)}) copy-start(s32[64,10]{0,1:T(8,128)} %param.35) | copy-start | bytes 7684
  19.8 6.7 %copy-start.10 = (s32[64,10]{0,1:T(8,128)S(1)}, s32[64,10]{0,1:T(8,128)}, u32[]{:S(2)}) copy-start(s32[64,10]{0,1:T(8,128)} %param.34) | copy-start | bytes 7684
  19.8 6.7 %copy-start.12 = (s32[32]{0:T(128)S(1)}, s32[32]{0:T(128)}, u32[]{:S(2)}) copy-start(s32[32]{0:T(128)} %param.36) | copy-start | bytes 388
  19.8 6.9 %copy-start.13 = (f32[64]{0:T(128)S(1)}, f32[64]{0:T(128)}, u32[]{:S(2)}) copy-start(f32[64]{0:T(128)} %param.26) | copy-start | bytes 772
  19.8 7.0 %copy-start.11 = (f32[64]{0:T(128)S(1)}, f32[64]{0:T(128)}, u32[]{:S(2)}) copy-start(f32[64]{0:T(128)} %param.25) | copy-start | bytes 772
  19.8 7.1 %copy-start.14 = (s32[64]{0:T(128)S(1)}, s32[64]{0:T(128)}, u32[]{:S(2)}) copy-start(s32[64]{0:T(128)} %param.30) | copy-start | bytes 772
  19.9 7.1 %copy-start.5 = (bf16[64,64]{1,0:T(8,128)(2,1)S(1)}, bf16[64,64]{1,0:T(8,128)(2,1)}, u32[]{:S(2)}) copy-start(bf16[64,64]{1,0:T(8,128)(2,1)} %param.24) | copy-start | bytes 24580
  19.9 7.1 %copy-start.6 = (bf16[64,128]{1,0:T(8,128)(2,1)S(1)}, bf16[64,128]{1,0:T(8,128)(2,1)}, u32[]{:S(2)}) copy-start(bf16[64,128]{1,0:T(8,128)(2,1)} %param.23) | copy-start | bytes 49156
  23.7 103.1 %all-to-all-start = ((bf16[2,64,64,128]{3,2,0,1:T(8,128)(2,1)}), bf16[2,64,64,128]{3,2,0,1:T(8,128)(2,1)S(1)}, u32[]{:S(2)}, u32[]{:S(2)}) async-start(bf16[2,64,64,128]{3,2,0,1:T(8,128)(2,1)} %copy.97), calls=%async_computation | async-start | bytes 4194304 | tf_op jit(solution)/shard_map/all_to_all | solution.py:280
  128.4 2.6 copy-start.3
  133.4 21.6 %copy-start.2 = (bf16[64,4096]{1,0:T(8,128)(2,1)S(1)}, bf16[64,4096]{1,0:T(8,128)(2,1)}, u32[]{:S(2)}) copy-start(bf16[64,4096]{1,0:T(8,128)(2,1)} %param.20) | copy-start | bytes 1572868
  134.5 21.8 %copy-start.15 = (f32[64]{0:T(128)S(1)}, f32[64]{0:T(128)}, u32[]{:S(2)}) copy-start(f32[64]{0:T(128)} %param.27) | copy-start | bytes 772
  135.8 36.2 %all-to-all-start.2 = ((bf16[32,64,128]{2,1,0:T(8,128)(2,1)}), bf16[32,64,128]{2,1,0:T(8,128)(2,1)}, u32[]{:S(2)}, u32[]{:S(2)}) async-start(bf16[32,64,128]{2,1,0:T(8,128)(2,1)} %all_to_all.39), calls=%async_computation.2 | async-start | bytes 1048576 | tf_op jit(solution)/shard_map/all_to_all | solution.py:298
  160.1 13.6 %copy-start.8 = (f32[4096]{0:T(1024)S(1)}, f32[4096]{0:T(1024)}, u32[]{:S(2)}) copy-start(f32[4096]{0:T(1024)} %param.28) | copy-start | bytes 49156
  160.2 13.7 %copy-start.4 = (bf16[64,2048]{1,0:T(8,128)(2,1)S(1)}, bf16[64,2048]{1,0:T(8,128)(2,1)}, u32[]{:S(2)}) copy-start(bf16[64,2048]{1,0:T(8,128)(2,1)} %param.31) | copy-start | bytes 786436
  173.9 9.1 %copy-start.1 = (bf16[64,4096]{1,0:T(8,128)(2,1)}, bf16[64,4096]{1,0:T(8,128)(2,1)S(1)}, u32[]{:S(2)}) copy-start(bf16[64,4096]{1,0:T(8,128)(2,1)S(1)} %multiply_convert_fusion.2) | copy-start | bytes 1572868
  173.9 9.1 %copy-start.9 = (f32[2048]{0:T(1024)S(1)}, f32[2048]{0:T(1024)}, u32[]{:S(2)}) copy-start(f32[2048]{0:T(1024)} %param.33) | copy-start | bytes 24580
Sparse Core Ops, SparseCore 0:
  10.9 158.8 all-gather.1

commit v3 on v2

--- a/solution.py
+++ b/solution.py
@@ -27,9 +27,9 @@
     return result.astype(jnp.bfloat16)
 
 
-def state_terms(c_proj, cumulative, start_state):
+def state_terms(c_proj, start_state):
     product = jnp.einsum("rtn,rhpn->rthp", c_proj, start_state, preferred_element_type=jnp.float32)
-    return (product * jnp.exp(cumulative)[..., None]).astype(jnp.bfloat16)
+    return product.astype(jnp.bfloat16)
 
 
 def place(devices):
@@ -236,6 +236,84 @@
         ),
         name="expert_block",
     )(rows, gate_weight, up_weight, down_weight)
+
+
+def project_kernel(
+    planes, rows_ref, w_hbm, out_ref, weight, arriving, leaving, returned, load_sem, send_sem, recv_sem
+):
+    z, y, x, c = place(planes * 8)
+    depth = weight.shape[0]
+    load = pltpu.make_async_copy(w_hbm, weight, load_sem)
+    load.start()
+
+    def at(k):
+        return {"wide": ((lax.rem(z + k, planes) * 2 + y) * 2 + x) * 2 + c}
+
+    def columns(k):
+        first = lax.rem(z + k, planes) * depth
+        return pl.ds(pl.multiple_of(first, depth), depth)
+
+    def send(src, dst, kind, k):
+        copy = pltpu.make_async_remote_copy(
+            src_ref=src,
+            dst_ref=dst.at[planes - k],
+            send_sem=send_sem.at[kind, k],
+            recv_sem=recv_sem.at[kind, planes - k],
+            device_id=at(k),
+            device_id_type=MESH,
+        )
+        copy.start()
+        return copy
+
+    def arrived(ref, kind, slot):
+        pltpu.make_async_copy(ref, ref, recv_sem.at[kind, slot]).wait()
+
+    barrier = pltpu.get_barrier_semaphore()
+    for k in range(1, planes):
+        pl.semaphore_signal(barrier, inc=1, device_id=at(k), device_id_type=MESH)
+    pl.semaphore_wait(barrier, planes - 1)
+
+    started = []
+    for k in range(planes - 1, 0, -1):
+        started.append(send(rows_ref.at[:, columns(k)], arriving, 0, k))
+    load.wait()
+    total = jnp.dot(rows_ref[:, columns(0)], weight[...], preferred_element_type=jnp.float32)
+    out_ref[...] = total
+    for k in range(1, planes):
+        arrived(arriving.at[k], 0, k)
+        part = jnp.dot(arriving[k], weight[...], preferred_element_type=jnp.float32)
+        leaving[k] = part.astype(leaving.dtype)
+        started.append(send(leaving.at[k], returned, 1, k))
+    for k in range(1, planes):
+        arrived(returned.at[k], 1, k)
+        out_ref[...] += returned[k].astype(jnp.float32)
+    for copy in started:
+        copy.wait_send()
+
+
+def project_block(rows, weight, devices):
+    planes = devices // 8
+    count = rows.shape[0]
+    depth, width = weight.shape
+    return pl.pallas_call(
+        functools.partial(project_kernel, planes),
+        out_shape=jax.ShapeDtypeStruct((count, width), jnp.float32),
+        in_specs=[pl.BlockSpec(memory_space=pltpu.VMEM), pl.BlockSpec(memory_space=pl.ANY)],
+        out_specs=pl.BlockSpec(memory_space=pltpu.VMEM),
+        scratch_shapes=[
+            pltpu.VMEM((depth, width), jnp.bfloat16),
+            pltpu.VMEM((planes, count, depth), jnp.bfloat16),
+            pltpu.VMEM((planes, count, width), jnp.bfloat16),
+            pltpu.VMEM((planes, count, width), jnp.bfloat16),
+            pltpu.SemaphoreType.DMA,
+            pltpu.SemaphoreType.DMA((2, planes)),
+            pltpu.SemaphoreType.DMA((2, planes)),
+        ],
+        compiler_params=pltpu.CompilerParams(
+            collective_id=1, has_side_effects=True, vmem_limit_bytes=40 * 1024 * 1024
+        ),
+        name="project_block",
+    )(rows, weight)
 
 
 def head_steps(raw_steps, bias_part, rate_part, requests):
@@ -275,8 +353,8 @@
     state_size = ssd_b.shape[1]
     req_local = tok_dev // SEQ
     rates = -jnp.exp(a_log)
-    bias_part = lax.dynamic_slice_in_dim(dt_bias, my_index * per_dev, per_dev)
-    rate_part = lax.dynamic_slice_in_dim(rates, my_index * per_dev, per_dev)
+    members = [list(range(first, first + 8)) for first in range(0, devices, 8)]
+    w_plane = lax.all_gather(w_out, "wide", axis=0, tiled=True, axis_index_groups=members)
     by_heads = lax.all_to_all(cache_state, "wide", split_axis=1, concat_axis=0, tiled=True)
     start_state = jnp.take(by_heads, cache_owner, axis=0)
     requests = cache_owner.shape[0]
@@ -292,9 +370,7 @@
     )
     intra = intra.reshape(tok_dev, heads_all * head_dim)
     c_all = lax.all_gather(ssd_c, "wide", axis=0, tiled=True)
-    head_raw = lax.all_to_all(dt_raw, "wide", split_axis=1, concat_axis=0, tiled=True)
-    step_size, cumulative = head_steps(head_raw, bias_part, rate_part, requests)
-    carried_head = state_terms(c_all.reshape(requests, SEQ, state_size), cumulative, start_state)
+    carried_head = state_terms(c_all.reshape(requests, SEQ, state_size), start_state)
     carried = lax.all_to_all(
         carried_head.reshape(tokens_all, per_dev * head_dim),
         "wide",
@@ -302,17 +378,15 @@
         concat_axis=1,
         tiled=True,
     )
-    mixed = intra.astype(jnp.float32) + carried.astype(jnp.float32)
+    decayed = carried.astype(jnp.float32).reshape(req_local, SEQ, heads_all, head_dim)
+    decayed = decayed * jnp.exp(local_cum)[..., None]
+    mixed = intra.astype(jnp.float32) + decayed.reshape(tok_dev, heads_all * head_dim)
     gated = mixed * jax.nn.silu(ssd_z.astype(jnp.float32))
     ssd_out = (
         gated * lax.rsqrt(jnp.mean(gated * gated, axis=-1, keepdims=True) + 1e-05) * norm_gain
     ).astype(jnp.bfloat16)
     width = resid.shape[1]
-    projected = jnp.dot(
-        ssd_out,
-        lax.all_gather(w_out, "wide", axis=0, tiled=True),
-        preferred_element_type=jnp.float32,
-    )
+    projected = project_block(ssd_out, w_plane, devices)
     wide_moe = resid.astype(jnp.float32) + projected
     normed = (
         wide_moe

time: 289 us -> 273 us (0.945)
  Pallas kernels: 95.8 us -> 137 us
  blocking collectives: 96.1 us -> 71.7 us
  starting transfers between devices: 29 us -> 13.8 us
  matrix products: 13.5 us -> 4.17 us
  waiting for transfers between devices: 16.3 us -> 8.51 us
    pallas_call x0 -> x1, Pallas kernels: none -> 37.8 us  [project_block(): pl.pallas_call(functools.partial(project_kernel, planes), out_shape=jax.S...]
    all_gather x1, blocking collectives: 96.1 us -> 71.7 us  [local(): c_all = lax.all_gather(ssd_c, 'wide', axis=0, tiled=True)]
    all_to_all x1, starting transfers between devices: 19 us -> 6.43 us  [local(): lax.all_to_all(carried_head.reshape(tokens_all, per_dev * head_dim), 'wid...]
    dot_general x1 -> x0, matrix products: 9.07 us -> none  [local(): jnp.dot(ssd_out, lax.all_gather(w_out, 'wide', axis=0, tiled=True), prefe...]
    all_to_all x1 -> x0, starting transfers between devices: 7.3 us -> none  [local(): lax.all_to_all(dt_raw, 'wide', split_axis=1, concat_axis=0, tiled=True)]
    all_to_all x1, starting transfers between devices: 2.73 us -> 7.3 us  [local(): lax.all_to_all(cache_state, 'wide', split_axis=1, concat_axis=0, tiled=True)]
    all_to_all x1, waiting for transfers between devices: 11.8 us -> 7.8 us  [local(): lax.all_to_all(carried_head.reshape(tokens_all, per_dev * head_dim), 'wid...]
    all_to_all x1 -> x0, waiting for transfers between devices: 3.82 us -> none  [local(): lax.all_to_all(dt_raw, 'wide', split_axis=1, concat_axis=0, tiled=True)]
  transfers between devices with their start and end apart: 4 -> 3, of which waited for: 2 -> 1; matrix products, arithmetic and copies ran while one was open for 8% -> 8% of each run, Pallas kernels for 0% -> 0%
where the time goes in v3:
time: 273 us; the launch traced here: 272 us
  Pallas kernels  137 us (50%)
  blocking collectives  71.7 us (26%)
  local copies, waits for them, and re-layouts  20.1 us (7%)
  between operations  14.4 us (5%)
  starting transfers between devices  13.8 us (5%)
  waiting for transfers between devices  8.51 us (3%)
  matrix products  4.17 us (2%)
  other arithmetic  2.8 us (1%)
    pallas_call x1, Pallas kernels, expert_block(): pl.pallas_call(functools.partial(expert_kernel, planes, devices), out_sha...  98.9 us
    all_gather x1, blocking collectives, local(): c_all = lax.all_gather(ssd_c, 'wide', axis=0, tiled=True)  71.7 us
    pallas_call x1, Pallas kernels, project_block(): pl.pallas_call(functools.partial(project_kernel, planes), out_shape=jax.S...  37.8 us
    all_to_all x1, waiting for transfers between devices, local(): lax.all_to_all(carried_head.reshape(tokens_all, per_dev * head_dim), 'wid...  7.8 us
    all_to_all x1, starting transfers between devices, local(): lax.all_to_all(cache_state, 'wide', split_axis=1, concat_axis=0, tiled=True)  7.3 us
    unnamed x34, local copies, waits for them, and re-layouts  7.25 us
    all_to_all x1, starting transfers between devices, local(): lax.all_to_all(carried_head.reshape(tokens_all, per_dev * head_dim), 'wid...  6.43 us
  transfers between devices with their start and end apart: 3, of which 1 were waited for; matrix products, arithmetic and copies ran while one was open for 8% of the time, Pallas kernels for 0%

profile of v3, /device:TPU:0, one launch (start us, length us, event | category | flops | bytes accessed | tf_op | source)
XLA Modules:
  0.0 272.1 jit_solution(17904842679748685539)
XLA Ops:
  7.2 0.0 copy-start
  7.2 0.0 all-gather.2.cloned.1.call-start
  7.2 0.7 all-gather.2.cloned.1.call-update
  7.9 3.1 %copy.81 = bf16[2,64,64,128]{3,2,0,1:T(8,128)(2,1)} copy(bf16[2,64,64,128]{3,2,1,0:T(8,128)(2,1)} %param.29) | data formatting | bytes 4194304 | tf_op args[9]
  11.1 0.0 copy-start.6
  11.1 0.0 copy-start.10
  11.1 0.0 copy-start.12
  11.1 0.0 copy-start.14
  11.1 0.0 copy-start.8
  11.1 0.0 copy-start.11
  11.1 0.0 copy-start.5
  11.1 7.3 %all-to-all-start = ((bf16[2,64,64,128]{3,2,0,1:T(8,128)(2,1)}), bf16[2,64,64,128]{3,2,0,1:T(8,128)(2,1)S(1)}, u32[]{:S(2)}, u32[]{:S(2)}) async-start(bf16[2,64,64,128]{3,2,0,1:T(8,128)(2,1)} %copy.81), calls=%async_computation | async-start | bytes 4194304 | tf_op jit(solution)/shard_map/all_to_all | solution.py:358
  18.4 0.0 copy-done.6
  18.5 0.0 copy-done.10
  18.5 0.0 copy-done.12
  18.5 0.1 select_reduce_fusion.1
  18.6 0.1 copy.87
  18.7 0.0 copy-done.13
  18.8 0.0 copy-done.14
  18.8 0.0 copy-done.8
  18.8 0.0 copy-done.11
  18.8 0.0 copy-done.5
  18.9 71.7 %all_gather.6 = bf16[2048,128]{1,0:T(8,128)(2,1)S(1)} all-gather(bf16[64,128]{1,0:T(8,128)(2,1)S(1)} %copy-done.5), channel_id=1, replica_groups=mesh['group'=1,'wide'=32] {'wide'}, dimensions={0}, use_global_device_ids=true | all-gather | bytes 540672 | tf_op jit(solution)/shard_map/all_gather | solution.py:372
  90.5 0.0 all-to-all-done
  90.5 1.6 copy.83
  92.1 2.5 gather_fusion
  94.7 2.1 fusion.8
  96.8 0.0 copy-start.4
  96.8 1.1 copy.84
  97.9 0.0 copy-start.15
  97.9 1.3 all_to_all.27
  99.2 6.4 %all-to-all-start.1 = ((bf16[32,64,128]{2,1,0:T(8,128)(2,1)}), bf16[32,64,128]{2,1,0:T(8,128)(2,1)}, u32[]{:S(2)}, u32[]{:S(2)}) async-start(bf16[32,64,128]{2,1,0:T(8,128)(2,1)} %all_to_all.27), calls=%async_computation.1 | async-start | bytes 1048576 | tf_op jit(solution)/shard_map/all_to_all | solution.py:374
  105.6 0.1 reduce_window_sum.11
  105.7 0.1 copy.75
  105.8 0.1 copy.77
  105.9 0.0 copy-done.4
  105.9 1.1 reshape.74
  107.0 0.0 copy-done
  107.0 0.1 fusion.27
  107.1 0.0 copy-done.15
  107.1 1.9 fusion.4
  109.1 1.2 copy.80
  110.3 0.7 reshape.76
  111.0 0.6 mul.96
  111.6 1.6 mul.97
  113.2 0.1 copy.88
  113.3 0.0 copy-start.7
  113.3 7.8 %all-to-all-done.1 = bf16[32,64,128]{2,1,0:T(8,128)(2,1)} async-done(((bf16[32,64,128]{2,1,0:T(8,128)(2,1)}), bf16[32,64,128]{2,1,0:T(8,128)(2,1)}, u32[]{:S(2)}, u32[]{:S(2)}) %all-to-all-start.1) | async-done | bytes 524320 | tf_op jit(solution)/shard_map/all_to_all | solution.py:374
  121.1 2.0 multiply_reduce_fusion
  123.2 0.0 copy-done.7
  123.2 0.2 multiply_convert_fusion.2.rows_ref
  123.4 0.0 copy-start.2
  123.4 0.0 all-gather.2.cloned.1.call-done.w_hbm
  123.4 0.0 copy-start.1
  123.4 2.3 copy-done.1
  125.8 37.8 %project_block.1 = f32[64,2048]{1,0:T(8,128)S(1)} custom-call(bf16[64,4096]{1,0:T(8,128)(2,1)S(1)} %multiply_convert_fusion.2.rows_ref, bf16[1024,2048]{1,0:T(8,128)(2,1)S(1)} %copy-done.1), custom_call_target="tpu_custom_call" | custom-call | tf_op jit(solution)/shard_map/project_block/pallas_call | solution.py:298
  163.6 0.0 copy-done.2
  163.6 0.0 copy-done.3
  163.6 0.2 multiply_reduce_fusion.1
  163.8 0.0 copy-done.9
  163.8 0.1 multiply_convert_fusion.3
  163.9 0.8 concatenate.3.rows_ref
  164.7 98.9 %expert_block.1 = bf16[64,2048]{1,0:T(8,128)(2,1)} custom-call(bf16[64,2176]{1,0:T(8,128)(2,1)} %concatenate.3.rows_ref, bf16[2048,384]{1,0:T(8,128)(2,1)} %bitcast.47, bf16[2048,384]{1,0:T(8,128)(2,1)} %bitcast.48, bf16[384,2048]{1,0:T(8,128)(2,1)} %bitcast.49), custom_call_target="tpu_custom_call" | custom-call | tf_op jit(solution)/shard_map/expert_block/pallas_call | solution.py:214
  263.6 1.7 copy.97
  (19 shorter events, 0.2 us)
Async XLA Ops:
  7.2 99.8 %copy-start = (bf16[64,128]{1,0:T(8,128)(2,1)S(1)}, bf16[64,128]{1,0:T(8,128)(2,1)}, u32[]{:S(2)}) copy-start(bf16[64,128]{1,0:T(8,128)(2,1)} %param.22) | copy-start | bytes 49156
  7.2 116.2 %all-gather.2.cloned.1.call-start = ((), (), s32[]{:S(2)}) async-start(), calls=%async_computation.2 | async-start | bytes 4718592 | tf_op jit(solution)/shard_map/all_gather | solution.py:357
  11.1 7.4 %copy-start.6 = (s32[64,10]{0,1:T(8,128)S(1)}, s32[64,10]{0,1:T(8,128)}, u32[]{:S(2)}) copy-start(s32[64,10]{0,1:T(8,128)} %param.35) | copy-start | bytes 7684
  11.1 7.4 %copy-start.10 = (s32[64,10]{0,1:T(8,128)S(1)}, s32[64,10]{0,1:T(8,128)}, u32[]{:S(2)}) copy-start(s32[64,10]{0,1:T(8,128)} %param.34) | copy-start | bytes 7684
  11.1 7.4 %copy-start.12 = (s32[32]{0:T(128)S(1)}, s32[32]{0:T(128)}, u32[]{:S(2)}) copy-start(s32[32]{0:T(128)} %param.36) | copy-start | bytes 388
  11.1 7.7 %copy-start.13 = (s32[64]{0:T(128)S(1)}, s32[64]{0:T(128)}, u32[]{:S(2)}) copy-start(s32[64]{0:T(128)} %param.30) | copy-start | bytes 772
  11.1 7.7 %copy-start.14 = (f32[64]{0:T(128)S(1)}, f32[64]{0:T(128)}, u32[]{:S(2)}) copy-start(f32[64]{0:T(128)} %param.26) | copy-start | bytes 772
  11.1 7.7 %copy-start.8 = (bf16[64,64]{1,0:T(8,128)(2,1)S(1)}, bf16[64,64]{1,0:T(8,128)(2,1)}, u32[]{:S(2)}) copy-start(bf16[64,64]{1,0:T(8,128)(2,1)} %param.24) | copy-start | bytes 24580
  11.1 7.7 %copy-start.11 = (f32[64]{0:T(128)S(1)}, f32[64]{0:T(128)}, u32[]{:S(2)}) copy-start(f32[64]{0:T(128)} %param.25) | copy-start | bytes 772
  11.1 7.7 %copy-start.5 = (bf16[64,128]{1,0:T(8,128)(2,1)S(1)}, bf16[64,128]{1,0:T(8,128)(2,1)}, u32[]{:S(2)}) copy-start(bf16[64,128]{1,0:T(8,128)(2,1)} %param.23) | copy-start | bytes 49156
  11.1 79.4 %all-to-all-start = ((bf16[2,64,64,128]{3,2,0,1:T(8,128)(2,1)}), bf16[2,64,64,128]{3,2,0,1:T(8,128)(2,1)S(1)}, u32[]{:S(2)}, u32[]{:S(2)}) async-start(bf16[2,64,64,128]{3,2,0,1:T(8,128)(2,1)} %copy.81), calls=%async_computation | async-start | bytes 4194304 | tf_op jit(solution)/shard_map/all_to_all | solution.py:358
  96.8 9.1 %copy-start.4 = (bf16[64,4096]{1,0:T(8,128)(2,1)S(1)}, bf16[64,4096]{1,0:T(8,128)(2,1)}, u32[]{:S(2)}) copy-start(bf16[64,4096]{1,0:T(8,128)(2,1)} %param.20) | copy-start | bytes 1572868
  97.9 9.3 %copy-start.15 = (f32[64]{0:T(128)S(1)}, f32[64]{0:T(128)}, u32[]{:S(2)}) copy-start(f32[64]{0:T(128)} %param.27) | copy-start | bytes 772
  99.2 22.0 %all-to-all-start.1 = ((bf16[32,64,128]{2,1,0:T(8,128)(2,1)}), bf16[32,64,128]{2,1,0:T(8,128)(2,1)}, u32[]{:S(2)}, u32[]{:S(2)}) async-start(bf16[32,64,128]{2,1,0:T(8,128)(2,1)} %all_to_all.27), calls=%async_computation.1 | async-start | bytes 1048576 | tf_op jit(solution)/shard_map/all_to_all | solution.py:374
  113.3 9.9 %copy-start.7 = (f32[4096]{0:T(1024)S(1)}, f32[4096]{0:T(1024)}, u32[]{:S(2)}) copy-start(f32[4096]{0:T(1024)} %param.28) | copy-start | bytes 49156
  123.4 40.2 %copy-start.2 = (bf16[64,4096]{1,0:T(8,128)(2,1)}, bf16[64,4096]{1,0:T(8,128)(2,1)S(1)}, u32[]{:S(2)}) copy-start(bf16[64,4096]{1,0:T(8,128)(2,1)S(1)} %multiply_convert_fusion.2.rows_ref) | copy-start | bytes 1572868
  123.4 2.4 copy-start.1
  125.8 37.8 %copy-start.3 = (bf16[64,2048]{1,0:T(8,128)(2,1)S(1)}, bf16[64,2048]{1,0:T(8,128)(2,1)}, u32[]{:S(2)}) copy-start(bf16[64,2048]{1,0:T(8,128)(2,1)} %param.31) | copy-start | bytes 786436
  125.8 38.0 %copy-start.9 = (f32[2048]{0:T(1024)S(1)}, f32[2048]{0:T(1024)}, u32[]{:S(2)}) copy-start(f32[2048]{0:T(1024)} %param.33) | copy-start | bytes 24580
Sparse Core Ops, SparseCore 0:
  9.9 59.9 all-gather.1

commit v4 on v3

--- a/solution.py
+++ b/solution.py
@@ -187,7 +187,7 @@
 
     stages = [spread_1, spread_2, spread_3, run, sum_1, sum_2, sum_3]
     for tick in range(planes + len(stages) - 1):
-        for number in reversed(range(len(stages))):
+        for number in (1, 0, 6, 5, 4, 3, 2):
             if 0 <= tick - number < planes:
                 stages[number](tick - number)
 
@@ -354,8 +354,9 @@
     req_local = tok_dev // SEQ
     rates = -jnp.exp(a_log)
     members = [list(range(first, first + 8)) for first in range(0, devices, 8)]
+    by_heads = lax.all_to_all(cache_state, "wide", split_axis=1, concat_axis=0, tiled=True)
+    by_heads, w_out = lax.optimization_barrier((by_heads, w_out))
     w_plane = lax.all_gather(w_out, "wide", axis=0, tiled=True, axis_index_groups=members)
-    by_heads = lax.all_to_all(cache_state, "wide", split_axis=1, concat_axis=0, tiled=True)
     start_state = jnp.take(by_heads, cache_owner, axis=0)
     requests = cache_owner.shape[0]
     tokens_all = requests * SEQ

time: 273 us -> 290 us (1.062)
  blocking collectives: 71.7 us -> 97.3 us
  starting transfers between devices: 13.8 us -> 3.37 us
  Pallas kernels: 137 us -> 140 us
    all_to_all x0 -> x1, blocking collectives: none -> 55.8 us  [local(): lax.all_to_all(cache_state, 'wide', split_axis=1, concat_axis=0, tiled=True)]
    all_gather x1, blocking collectives: 71.7 us -> 41.5 us  [local(): c_all = lax.all_gather(ssd_c, 'wide', axis=0, tiled=True)]
    all_to_all x1 -> x0, starting transfers between devices: 7.3 us -> none  [local(): lax.all_to_all(cache_state, 'wide', split_axis=1, concat_axis=0, tiled=True)]
    pallas_call x1, Pallas kernels: 98.9 us -> 103 us  [expert_block(): pl.pallas_call(functools.partial(expert_kernel, planes, devices), out_sha...]
    all_to_all x1, starting transfers between devices: 6.43 us -> 3.33 us  [local(): lax.all_to_all(carried_head.reshape(tokens_all, per_dev * head_dim), 'wid...]
  transfers between devices with their start and end apart: 3 -> 2, of which waited for: 1 -> 1; matrix products, arithmetic and copies ran while one was open for 8% -> 6% of each run, Pallas kernels for 0% -> 0%
where the time goes in v4:
time: 290 us; the launch traced here: 289 us
  Pallas kernels  140 us (48%)
  blocking collectives  97.3 us (34%)
  local copies, waits for them, and re-layouts  17.4 us (6%)
  between operations  14.4 us (5%)
  waiting for transfers between devices  7.83 us (3%)
  matrix products  5.75 us (2%)
  starting transfers between devices  3.37 us (1%)
    pallas_call x1, Pallas kernels, expert_block(): pl.pallas_call(functools.partial(expert_kernel, planes, devices), out_sha...  103 us
    all_to_all x1, blocking collectives, local(): lax.all_to_all(cache_state, 'wide', split_axis=1, concat_axis=0, tiled=True)  55.8 us
    all_gather x1, blocking collectives, local(): c_all = lax.all_gather(ssd_c, 'wide', axis=0, tiled=True)  41.5 us
    pallas_call x1, Pallas kernels, project_block(): pl.pallas_call(functools.partial(project_kernel, planes), out_shape=jax.S...  37.8 us
    all_to_all x1, waiting for transfers between devices, local(): lax.all_to_all(carried_head.reshape(tokens_all, per_dev * head_dim), 'wid...  7.79 us
    unnamed x34, local copies, waits for them, and re-layouts  6.3 us
  transfers between devices with their start and end apart: 2, of which 1 were waited for; matrix products, arithmetic and copies ran while one was open for 6% of the time, Pallas kernels for 0%

profile of v4, /device:TPU:0, one launch (start us, length us, event | category | flops | bytes accessed | tf_op | source)
XLA Modules:
  0.0 289.2 jit_solution(17564750231489015984)
XLA Ops:
  7.2 0.0 copy-start
  7.2 0.0 all-gather.2.cloned.1.call-start
  7.2 1.8 copy.81
  9.0 55.8 %all_to_all.31 = bf16[2,64,64,128]{3,2,0,1:T(8,128)(2,1)S(1)} all-to-all(bf16[2,64,64,128]{3,2,0,1:T(8,128)(2,1)S(1)} %copy.81), channel_id=1, replica_groups=mesh['group'=1,'wide'=32] {'wide'}, dimensions={1} | all-to-all | bytes 4194304 | tf_op jit(solution)/shard_map/all_to_all | solution.py:357
  64.8 0.0 copy-start.6
  64.8 0.0 copy-start.10
  64.8 0.0 copy-start.12
  64.8 0.0 copy-start.13
  64.8 0.0 copy-start.14
  64.8 0.0 copy-start.8
  64.8 0.0 copy-start.11
  64.8 0.0 copy-start.5
  64.9 0.2 copy.83
  65.0 0.0 all-gather.2.cloned.1.call-update
  65.1 0.4 copy-done.6
  65.5 0.0 copy-done.10
  65.5 0.0 copy-done.12
  65.5 0.1 select_reduce_fusion.1
  65.7 0.1 copy.87
  65.8 0.0 copy-done.13
  65.8 0.0 copy-done.14
  65.8 0.0 copy-done.8
  65.9 0.0 copy-done.11
  65.9 0.0 copy-done.5
  65.9 41.5 %all_gather.6 = bf16[2048,128]{1,0:T(8,128)(2,1)S(1)} all-gather(bf16[64,128]{1,0:T(8,128)(2,1)S(1)} %copy-done.5), channel_id=1, replica_groups=mesh['group'=1,'wide'=32] {'wide'}, dimensions={0}, use_global_device_ids=true | all-gather | bytes 540672 | tf_op jit(solution)/shard_map/all_gather | solution.py:373
  107.4 2.1 gather_fusion
  109.5 3.7 %fusion.8 = bf16[64,32,2,64]{3,1,2,0:T(8,128)(2,1)S(1)} fusion(bf16[64,32,128,1]{2,1,3,0:T(8,128)(2,1)S(1)} %bitcast.50, bf16[64,2,64,128]{3,2,1,0:T(8,128)(2,1)} %gather_fusion, pred[64]{0:T(512)(128)(4,1)S(1)} %compare_and_fusion), kind=kOutput, calls=%fused_computation.9 | convolution fusion | flops 68419584 | bytes 3145792 | tf_op jit(solution)/shard_map/rtn,rhpn->rthp/dot_general | solution.py:31
  113.2 0.0 copy-start.4
  113.3 1.1 copy.84
  114.3 0.0 copy-start.15
  114.4 1.3 all_to_all.27
  115.6 3.3 %all-to-all-start.1 = ((bf16[32,64,128]{2,1,0:T(8,128)(2,1)}), bf16[32,64,128]{2,1,0:T(8,128)(2,1)}, u32[]{:S(2)}, u32[]{:S(2)}) async-start(bf16[32,64,128]{2,1,0:T(8,128)(2,1)} %all_to_all.27), calls=%async_computation.1 | async-start | bytes 1048576 | tf_op jit(solution)/shard_map/all_to_all | solution.py:375
  119.0 0.1 reduce_window_sum.11
  119.1 0.1 copy.75
  119.1 0.1 copy.77
  119.2 0.0 copy-done.4
  119.2 1.1 reshape.74
  120.4 0.0 copy-done
  120.4 0.1 fusion.27
  120.5 0.0 copy-done.15
  120.5 1.9 fusion.4
  122.5 1.2 copy.80
  123.7 0.7 reshape.76
  124.3 0.6 mul.96
  124.9 1.6 mul.97
  126.6 0.1 copy.88
  126.7 0.0 copy-start.7
  126.7 7.8 %all-to-all-done.1 = bf16[32,64,128]{2,1,0:T(8,128)(2,1)} async-done(((bf16[32,64,128]{2,1,0:T(8,128)(2,1)}), bf16[32,64,128]{2,1,0:T(8,128)(2,1)}, u32[]{:S(2)}, u32[]{:S(2)}) %all-to-all-start.1) | async-done | bytes 524320 | tf_op jit(solution)/shard_map/all_to_all | solution.py:375
  134.5 2.0 multiply_reduce_fusion
  136.5 0.0 copy-done.7
  136.6 0.2 multiply_convert_fusion.2.rows_ref
  136.7 0.0 copy-start.2
  136.8 0.0 all-gather.2.cloned.1.call-done.w_hbm
  136.8 0.0 copy-start.1
  136.8 2.3 copy-done.1
  139.1 37.8 %project_block.1 = f32[64,2048]{1,0:T(8,128)S(1)} custom-call(bf16[64,4096]{1,0:T(8,128)(2,1)S(1)} %multiply_convert_fusion.2.rows_ref, bf16[1024,2048]{1,0:T(8,128)(2,1)S(1)} %copy-done.1), custom_call_target="tpu_custom_call" | custom-call | tf_op jit(solution)/shard_map/project_block/pallas_call | solution.py:298
  176.9 0.0 copy-done.2
  176.9 0.0 copy-done.3
  177.0 0.2 multiply_reduce_fusion.1
  177.1 0.0 copy-done.9
  177.1 0.1 multiply_convert_fusion.3
  177.3 0.8 concatenate.3.rows_ref
  178.1 102.6 %expert_block.1 = bf16[64,2048]{1,0:T(8,128)(2,1)} custom-call(bf16[64,2176]{1,0:T(8,128)(2,1)} %concatenate.3.rows_ref, bf16[2048,384]{1,0:T(8,128)(2,1)} %bitcast.47, bf16[2048,384]{1,0:T(8,128)(2,1)} %bitcast.48, bf16[384,2048]{1,0:T(8,128)(2,1)} %bitcast.49), custom_call_target="tpu_custom_call" | custom-call | tf_op jit(solution)/shard_map/expert_block/pallas_call | solution.py:214
  280.7 1.7 copy.97
  (18 shorter events, 0.2 us)
Async XLA Ops:
  7.2 113.2 %copy-start = (bf16[64,128]{1,0:T(8,128)(2,1)S(1)}, bf16[64,128]{1,0:T(8,128)(2,1)}, u32[]{:S(2)}) copy-start(bf16[64,128]{1,0:T(8,128)(2,1)} %param.22) | copy-start | bytes 49156
  7.2 129.6 %all-gather.2.cloned.1.call-start = ((), (), s32[]{:S(2)}) async-start(), calls=%async_computation.2 | async-start | bytes 4718592 | tf_op jit(solution)/shard_map/all_gather | solution.py:359
  64.8 0.7 copy-start.6
  64.8 0.7 copy-start.10
  64.8 0.7 copy-start.12
  64.8 1.0 copy-start.13
  64.8 1.0 copy-start.14
  64.8 1.0 copy-start.8
  64.8 1.0 copy-start.11
  64.8 1.1 copy-start.5
  113.2 6.0 %copy-start.4 = (bf16[64,4096]{1,0:T(8,128)(2,1)S(1)}, bf16[64,4096]{1,0:T(8,128)(2,1)}, u32[]{:S(2)}) copy-start(bf16[64,4096]{1,0:T(8,128)(2,1)} %param.20) | copy-start | bytes 1572868
  114.3 6.2 %copy-start.15 = (f32[64]{0:T(128)S(1)}, f32[64]{0:T(128)}, u32[]{:S(2)}) copy-start(f32[64]{0:T(128)} %param.27) | copy-start | bytes 772
  115.6 18.9 %all-to-all-start.1 = ((bf16[32,64,128]{2,1,0:T(8,128)(2,1)}), bf16[32,64,128]{2,1,0:T(8,128)(2,1)}, u32[]{:S(2)}, u32[]{:S(2)}) async-start(bf16[32,64,128]{2,1,0:T(8,128)(2,1)} %all_to_all.27), calls=%async_computation.1 | async-start | bytes 1048576 | tf_op jit(solution)/shard_map/all_to_all | solution.py:375
  126.7 9.9 %copy-start.7 = (f32[4096]{0:T(1024)S(1)}, f32[4096]{0:T(1024)}, u32[]{:S(2)}) copy-start(f32[4096]{0:T(1024)} %param.28) | copy-start | bytes 49156
  136.7 40.2 %copy-start.2 = (bf16[64,4096]{1,0:T(8,128)(2,1)}, bf16[64,4096]{1,0:T(8,128)(2,1)S(1)}, u32[]{:S(2)}) copy-start(bf16[64,4096]{1,0:T(8,128)(2,1)S(1)} %multiply_convert_fusion.2.rows_ref) | copy-start | bytes 1572868
  136.8 2.4 copy-start.1
  139.1 37.8 %copy-start.3 = (bf16[64,2048]{1,0:T(8,128)(2,1)S(1)}, bf16[64,2048]{1,0:T(8,128)(2,1)}, u32[]{:S(2)}) copy-start(bf16[64,2048]{1,0:T(8,128)(2,1)} %param.31) | copy-start | bytes 786436
  139.1 38.0 %copy-start.9 = (f32[2048]{0:T(1024)S(1)}, f32[2048]{0:T(1024)}, u32[]{:S(2)}) copy-start(f32[2048]{0:T(1024)} %param.33) | copy-start | bytes 24580
Sparse Core Ops, SparseCore 0:
  65.2 38.1 all-gather.1
